TPU v7x, 32 devices: a whole 2x2x4 slice. The times are simulated.
32 devices in a mesh: dp: 16 (over z, y, x), tensor: 2 (over core).
Axes of the slice: x: 2, y: 2, z: 4, core: 2. Of those that a mesh axis runs over, the one named last changes fastest.
Arguments:
- tokens: bfloat16 [16384, 1024], P(('dp', 'tensor')), may hold values from -6 to 6
- episode_lengths: int32 [16, 4], P('dp'), may hold values from 1 to 640, 1024 in all within a row
- attn_gain: float32 [1024], replicated, may hold values from 0.25 to 1.75
- attn_shift: float32 [1024], replicated, may hold values from -3 to 3
- proj_weight: bfloat16 [3, 1024, 1024], P(None, None, 'tensor'), may hold values from -0.1875 to 0.1875
- proj_bias: float32 [3, 1024], P(None, 'tensor'), may hold values from -2 to 2
- out_weight: bfloat16 [1024, 1024], P('tensor'), may hold values from -1.5 to 1.5
- out_bias: float32 [1024], replicated, may hold values from -2 to 2
- mlp_gain: float32 [1024], replicated, may hold values from 0.25 to 1.75
- mlp_shift: float32 [1024], replicated, may hold values from -3 to 3
- up_weight: bfloat16 [1024, 4096], P(None, 'tensor'), may hold values from -0.1875 to 0.1875
- up_bias: float32 [4096], P('tensor'), may hold values from -2 to 2
- down_weight: bfloat16 [4096, 1024], P('tensor'), may hold values from -0.1875 to 0.1875
- down_bias: float32 [1024], replicated, may hold values from -2 to 2
- cotangent: bfloat16 [16384, 1024], P(('dp', 'tensor')), may hold values from -6 to 6
Outputs:
- mixed: bfloat16 [16384, 1024], P(('dp', 'tensor'))
- grad_tokens: float32 [16384, 1024], P(('dp', 'tensor'))
- grad_attn_gain: float32 [1024], replicated
- grad_attn_shift: float32 [1024], replicated
- grad_proj_weight: float32 [3, 1024, 1024], P(None, 'dp', 'tensor')
- grad_proj_bias: float32 [3, 1024], replicated
- grad_out_weight: float32 [1024, 1024], P('tensor', 'dp')
- grad_out_bias: float32 [1024], replicated
- grad_mlp_gain: float32 [1024], replicated
- grad_mlp_shift: float32 [1024], replicated
- grad_up_weight: float32 [1024, 4096], P('dp', 'tensor')
- grad_up_bias: float32 [4096], replicated
- grad_down_weight: float32 [4096, 1024], P('tensor', 'dp')
- grad_down_bias: float32 [1024], replicated
Inputs may be any that keep to these rules, and one draw needn't show every extreme that they name: `episode_lengths`: each row lists the lengths of the 4 episodes of one pack in order; a row sums to 1024 and its largest entry is exactly 640.
All inputs are finite; a program needn't handle non-finite values.
Results may differ from a plain program's by a relative error of at most 0.017.
Values may be sent and summed in bfloat16 or wider, within the bound.
A program may use at most 192 MiB of HBM per device.

v0:
```python
import jax
import jax.numpy as jnp
from jax import lax
from jax.sharding import PartitionSpec as P

HEAD = 64
GRID = 16
FRAME = 258


epsilon = 1e-06


def layer_norm(values, gain, shift):
    centre = values - jnp.mean(values, axis=-1, keepdims=True)
    spread = jnp.mean(centre * centre, axis=-1, keepdims=True)
    return centre * lax.rsqrt(spread + epsilon) * gain + shift


def rotate(values, time_pos, row_pos, col_pos):
    head_width = values.shape[-1]
    side_width = 2 * (head_width // 6)
    pieces = []
    offset = 0
    for section, where_pos in (
        (head_width - 2 * side_width, time_pos),
        (side_width, row_pos),
        (side_width, col_pos),
    ):
        half_width = section // 2
        frequency = 10000.0 ** (-jnp.arange(half_width, dtype=jnp.float32) * 2.0 / section)
        angles = where_pos.astype(jnp.float32)[:, None] * frequency[None, :]
        cosine = jnp.cos(angles)[:, None, :]
        sine_part = jnp.sin(angles)[:, None, :]
        leading = values[..., offset : offset + half_width]
        second = values[..., offset + half_width : offset + section]
        pieces.append(leading * cosine - second * sine_part)
        pieces.append(second * cosine + leading * sine_part)
        offset = offset + section
    return jnp.concatenate(pieces, axis=-1)


def positions(lengths_row, count):
    ends = jnp.cumsum(lengths_row)
    starts = ends - lengths_row
    places = jnp.arange(count, dtype=jnp.int32)
    episode = jnp.sum((places[None, :] >= ends[:, None]).astype(jnp.int32), axis=0)
    member = episode[None, :] == jnp.arange(lengths_row.shape[0], dtype=jnp.int32)[:, None]
    begin = jnp.sum(jnp.where(member, starts[:, None], 0), axis=0)
    local_pos = places - begin
    frame_id = local_pos // FRAME
    within_frame = local_pos % FRAME
    patch_id = jnp.maximum(within_frame - 2, 0)
    row_pos = jnp.where(within_frame >= 2, patch_id // GRID, 0)
    col_pos = jnp.where(within_frame >= 2, patch_id % GRID, 0)
    return (episode, frame_id, row_pos, col_pos)


def gelu_exact(values):
    return jax.nn.gelu(values, approximate=False)


def rounded(values):
    return lax.optimization_barrier(values.astype(jnp.bfloat16)).astype(jnp.float32)


def on_device(
    tokens,
    episode_lengths,
    attn_gain,
    attn_shift,
    proj_weight,
    proj_bias,
    out_weight,
    out_bias,
    mlp_gain,
    mlp_shift,
    up_weight,
    up_bias,
    down_weight,
    down_bias,
    cotangent,
):
    tok_rows, width = tokens.shape
    ways = lax.axis_size("tensor")
    pack_rows = tok_rows * ways
    local_width = proj_weight.shape[2]
    local_heads = local_width // HEAD
    hidden_local = up_weight.shape[1]
    scale = HEAD ** (-0.5)
    episode, frame_id, row_pos, col_pos = positions(episode_lengths[0], pack_rows)
    block = min(512, pack_rows)
    block_count = pack_rows // block
    block_ids = jnp.arange(block_count, dtype=jnp.int32)
    tokens_wide = tokens.astype(jnp.float32)
    normed_one, norm_one_back = jax.vjp(layer_norm, tokens_wide, attn_gain, attn_shift)
    normed_full = lax.all_gather(normed_one.astype(jnp.bfloat16), "tensor", axis=0, tiled=True)
    project = (
        jnp.einsum("pd,cde->cpe", normed_full, proj_weight, preferred_element_type=jnp.float32)
        + proj_bias[:, None, :]
    )

    def rope_query(values):
        return rotate(values, frame_id, row_pos, col_pos) * scale

    def rope_key(values):
        return rotate(values, frame_id, row_pos, col_pos)

    queries_wide, query_back = jax.vjp(rope_query, project[0].reshape(pack_rows, local_heads, HEAD))
    keys_wide, key_back = jax.vjp(rope_key, project[1].reshape(pack_rows, local_heads, HEAD))
    queries = queries_wide.astype(jnp.bfloat16)
    key_rows = keys_wide.astype(jnp.bfloat16)
    value_rows = project[2].reshape(pack_rows, local_heads, HEAD).astype(jnp.bfloat16)

    def scores_for(start, q_block):
        episode_q = lax.dynamic_slice_in_dim(episode, start, block, 0)
        frame_q = lax.dynamic_slice_in_dim(frame_id, start, block, 0)
        scores = jnp.einsum("qhe,khe->hqk", q_block, key_rows, preferred_element_type=jnp.float32)
        allowed = (episode_q[:, None] == episode[None, :]) & (frame_id[None, :] <= frame_q[:, None])
        return jnp.where(allowed[None], scores, -1e30)

    def forward_block(index):
        start = index * block
        q_block = lax.dynamic_slice_in_dim(queries, start, block, 0)
        scores = scores_for(start, q_block)
        highest = jnp.max(scores, axis=-1, keepdims=True)
        raised = jnp.exp(scores - highest)
        total = jnp.sum(raised, axis=-1, keepdims=True)
        attention = raised / total
        result = jnp.einsum(
            "hqk,khe->qhe",
            attention.astype(jnp.bfloat16),
            value_rows,
            preferred_element_type=jnp.float32,
        )
        return (result, (highest + jnp.log(total))[..., 0])

    blocks, log_totals = lax.map(forward_block, block_ids)
    attended = blocks.reshape(pack_rows, local_width).astype(jnp.bfloat16)
    rows_now = lax.slice_in_dim(attended, 0, tok_rows * lax.axis_size("tensor"), axis=0)
    middle = tokens_wide + (
        lax.psum_scatter(
            jnp.dot(rows_now, out_weight, preferred_element_type=jnp.float32).astype(jnp.bfloat16),
            "tensor",
            scatter_dimension=0,
            tiled=True,
        ).astype(jnp.float32)
        + out_bias
    )
    normed_two, norm_two_back = jax.vjp(layer_norm, middle, mlp_gain, mlp_shift)
    normed_two_full = lax.all_gather(normed_two.astype(jnp.bfloat16), "tensor", axis=0, tiled=True)
    hidden = jnp.dot(normed_two_full, up_weight, preferred_element_type=jnp.float32) + up_bias
    active, gelu_back = jax.vjp(gelu_exact, hidden)
    active_low = active.astype(jnp.bfloat16)
    rows_now = lax.slice_in_dim(active_low, 0, tok_rows * lax.axis_size("tensor"), axis=0)
    mixed = (
        middle
        + (
            lax.psum_scatter(
                jnp.dot(rows_now, down_weight, preferred_element_type=jnp.float32).astype(
                    jnp.bfloat16
                ),
                "tensor",
                scatter_dimension=0,
                tiled=True,
            ).astype(jnp.float32)
            + down_bias
        )
    ).astype(jnp.bfloat16)
    cot_full = lax.all_gather(cotangent, "tensor", axis=0, tiled=True)
    grad_down_weight = jnp.einsum(
        "pf,pd->fd", active_low, cot_full, preferred_element_type=jnp.float32
    )
    grad_down_bias = jnp.sum(cotangent, axis=0, dtype=jnp.float32)
    grad_active = jnp.einsum("pd,fd->pf", cot_full, down_weight, preferred_element_type=jnp.float32)
    grad_hidden = gelu_back(grad_active)[0].astype(jnp.bfloat16)
    grad_up_weight = jnp.einsum(
        "pd,pf->df", normed_two_full, grad_hidden, preferred_element_type=jnp.float32
    )
    grad_up_bias = jnp.sum(grad_hidden, axis=0, dtype=jnp.float32)
    rows_now = lax.slice_in_dim(grad_hidden, 0, tok_rows * lax.axis_size("tensor"), axis=0)
    grad_normed_two = lax.psum_scatter(
        jnp.einsum("pf,df->pd", rows_now, up_weight, preferred_element_type=jnp.float32).astype(
            jnp.bfloat16
        ),
        "tensor",
        scatter_dimension=0,
        tiled=True,
    ).astype(jnp.float32)
    grad_middle_norm, grad_mlp_gain, grad_mlp_shift = norm_two_back(grad_normed_two)
    grad_middle = cotangent.astype(jnp.float32) + grad_middle_norm
    grad_branch = grad_middle.astype(jnp.bfloat16)
    grad_branch_full = lax.all_gather(grad_branch, "tensor", axis=0, tiled=True)
    grad_out_weight = jnp.einsum(
        "pe,pd->ed", attended, grad_branch_full, preferred_element_type=jnp.float32
    )
    grad_out_bias = jnp.sum(grad_branch, axis=0, dtype=jnp.float32)
    grad_attended = jnp.einsum(
        "pd,ed->pe", grad_branch_full, out_weight, preferred_element_type=jnp.float32
    )
    grad_attended = grad_attended.astype(jnp.bfloat16).reshape(pack_rows, local_heads, HEAD)

    def backward_block(carry, index):
        grad_keys, grad_values = carry
        start = index * block
        q_block = lax.dynamic_slice_in_dim(queries, start, block, 0)
        grad_out_block = lax.dynamic_slice_in_dim(grad_attended, start, block, 0)
        scores = scores_for(start, q_block)
        attention = jnp.exp(scores - log_totals[index][..., None])
        grad_attention = jnp.einsum(
            "qhe,khe->hqk", grad_out_block, value_rows, preferred_element_type=jnp.float32
        )
        inner = jnp.sum(attention * grad_attention, axis=-1, keepdims=True)
        grad_scores = (attention * (grad_attention - inner)).astype(jnp.bfloat16)
        grad_q_block = jnp.einsum(
            "hqk,khe->qhe", grad_scores, key_rows, preferred_element_type=jnp.float32
        )
        grad_keys = grad_keys + jnp.einsum(
            "hqk,qhe->khe", grad_scores, q_block, preferred_element_type=jnp.float32
        )
        grad_values = grad_values + jnp.einsum(
            "hqk,qhe->khe",
            attention.astype(jnp.bfloat16),
            grad_out_block,
            preferred_element_type=jnp.float32,
        )
        return ((grad_keys, grad_values), grad_q_block)

    zero_rows = jnp.zeros((pack_rows, local_heads, HEAD), jnp.float32)
    (grad_keys, grad_values), grad_queries = lax.scan(
        backward_block, (zero_rows, zero_rows), block_ids
    )
    grad_queries = rounded(grad_queries.reshape(pack_rows, local_heads, HEAD))
    grad_query_raw = query_back(grad_queries)[0]
    grad_key_raw = key_back(rounded(grad_keys))[0]
    grad_project = jnp.stack(
        [
            grad_query_raw.reshape(pack_rows, local_width),
            grad_key_raw.reshape(pack_rows, local_width),
            grad_values.reshape(pack_rows, local_width),
        ]
    ).astype(jnp.bfloat16)
    grad_proj_weight = jnp.einsum(
        "pd,cpe->cde", normed_full, grad_project, preferred_element_type=jnp.float32
    )
    grad_proj_bias = jnp.sum(grad_project, axis=1, dtype=jnp.float32)
    rows_now = grad_project
    grad_normed_one = lax.psum_scatter(
        jnp.einsum("cpe,cde->pd", rows_now, proj_weight, preferred_element_type=jnp.float32).astype(
            jnp.bfloat16
        ),
        "tensor",
        scatter_dimension=0,
        tiled=True,
    ).astype(jnp.float32)
    grad_input_norm, grad_attn_gain, grad_attn_shift = norm_one_back(grad_normed_one)
    grad_tokens = grad_middle + grad_input_norm
    grad_proj_weight, grad_out_weight, grad_up_weight, grad_down_weight = (
        lax.psum_scatter(grad_proj_weight, "dp", scatter_dimension=1, tiled=True),
        lax.psum_scatter(grad_out_weight, "dp", scatter_dimension=1, tiled=True),
        lax.psum_scatter(grad_up_weight, "dp", scatter_dimension=0, tiled=True),
        lax.psum_scatter(grad_down_weight, "dp", scatter_dimension=1, tiled=True),
    )
    position_here = lax.axis_index("tensor")
    full_proj_bias = lax.dynamic_update_slice_in_dim(
        jnp.zeros((3, local_width * ways), jnp.float32),
        grad_proj_bias,
        position_here * local_width,
        1,
    )
    full_up_bias = lax.dynamic_update_slice_in_dim(
        jnp.zeros((hidden_local * ways,), jnp.float32),
        grad_up_bias,
        position_here * hidden_local,
        0,
    )
    (
        grad_attn_gain,
        grad_attn_shift,
        full_proj_bias,
        grad_out_bias,
        grad_mlp_gain,
        grad_mlp_shift,
        full_up_bias,
        grad_down_bias,
    ) = lax.psum(
        (
            grad_attn_gain,
            grad_attn_shift,
            full_proj_bias,
            grad_out_bias,
            grad_mlp_gain,
            grad_mlp_shift,
            full_up_bias,
            grad_down_bias,
        ),
        ("dp", "tensor"),
    )
    return (
        mixed,
        grad_tokens,
        grad_attn_gain,
        grad_attn_shift,
        grad_proj_weight,
        full_proj_bias,
        grad_out_weight,
        grad_out_bias,
        grad_mlp_gain,
        grad_mlp_shift,
        grad_up_weight,
        full_up_bias,
        grad_down_weight,
        grad_down_bias,
    )


def solution(mesh):
    return jax.shard_map(
        on_device,
        mesh=mesh,
        in_specs=(
            P(("dp", "tensor"), None),
            P("dp", None),
            P(),
            P(),
            P(None, None, "tensor"),
            P(None, "tensor"),
            P("tensor", None),
            P(),
            P(),
            P(),
            P(None, "tensor"),
            P("tensor"),
            P("tensor", None),
            P(),
            P(("dp", "tensor"), None),
        ),
        out_specs=(
            P(("dp", "tensor"), None),
            P(("dp", "tensor"), None),
            P(),
            P(),
            P(None, "dp", "tensor"),
            P(),
            P("tensor", "dp"),
            P(),
            P(),
            P(),
            P("dp", "tensor"),
            P(),
            P("tensor", "dp"),
            P(),
        ),
        check_vma=False,
    )
```

profile of v0, /device:TPU:0, one launch (start us, length us, event | category | flops | bytes accessed | tf_op | source)
XLA Modules:
  0.0 1113.4 jit_solution(15539793570898769215)
XLA Ops:
  15.8 12.1 %all-gather.5.cloned.1.call-done = bf16[1024,1024]{1,0:T(8,128)(2,1)} async-done(((bf16[512,1024]{1,0:T(8,128)(2,1)}), bf16[1024,1024]{1,0:T(8,128)(2,1)}) %all-gather.5.cloned.1.call-update) | async-done | bytes 2097168 | tf_op jit(solution)/shard_map/all_gather | solution.py:97
  38.9 20.8 %concatenate.7 = f32[1024,8,64]{0,2,1:T(8,128)} concatenate(f32[1024,8,12]{0,2,1:T(8,128)} %get-tuple-element.335, f32[1024,8,12]{0,2,1:T(8,128)} %get-tuple-element.336, f32[1024,8,10]{0,2,1:T(8,128)} %get-tuple-element.329, f32[1024,8,10]{0,2,1:T(8,128)} %get-tuple-element.330, f32[1024,8,10]{0,2,1:T(8,128)} %get-tuple-element.317, f32[1024,8,10]{0,2,1:T(8,128)} %get-tuple-element.316), dimensions={2} | concatenate | bytes 4194304 | tf_op jit(solution)/shard_map/jvp()/concatenate | solution.py:40
  62.6 19.1 %concatenate.8 = bf16[1024,8,64]{0,2,1:T(8,128)(2,1)} concatenate(bf16[1024,8,12]{0,2,1:T(8,128)(2,1)} %get-tuple-element.315, bf16[1024,8,12]{0,2,1:T(8,128)(2,1)} %get-tuple-element.314, bf16[1024,8,10]{0,2,1:T(8,128)(2,1)} %get-tuple-element.327, bf16[1024,8,10]{0,2,1:T(8,128)(2,1)} %get-tuple-element.328, bf16[1024,8,10]{0,2,1:T(8,128)(2,1)} %get-tuple-element.311, ...), dimensions={2} | concatenate | bytes 2097152 | tf_op jit(solution)/shard_map/jvp()/concatenate | solution.py:40
  82.9 31.5 %while.27 = (s32[]{:T(128)}, bf16[2,512,8,64]{1,3,2,0:T(8,128)(2,1)}, f32[2,8,512]{2,1,0:T(8,128)S(1)}, s32[2]{0:T(128)S(1)}, s32[1024]{0:T(1024)S(1)}, /*index=...) while((s32[]{:T(128)}, ...), condition=%wide.region_8.9_spmd, body=%wide.region_5.8_spmd.sunk | while | flops 1113059328 | bytes 68833568 | solution.py:138
  120.8 10.9 reduce-scatter.8.cloned.1.call-done
  138.4 11.1 all-gather.7.cloned.1.call-done
  149.4 10.9 fusion.70
  162.7 28.4 %convert_reduce_fusion = (f32[2048]{0:T(1024)}, bf16[1024,2048]{1,0:T(8,128)(2,1)S(1)}, f32[1024,2048]{1,0:T(8,128)}) fusion(f32[1024,2048]{1,0:T(8,128)} %fusion.70, f32[2048]{0:T(1024)S(1)} %copy-done.46, bf16[1024,1024]{1,0:T(8,128)(2,1)} %all-gather.9.cloned.1.call-done, bf16[2048,1024]{1,0:T(8,128)(2,1)} %param.31), kind=kOutput, calls=%fused_computation.40 | convolution fusion | flops 4452251648 | bytes 27279360 | tf_op jit(solution)/shard_map/pd,fd->pf/dot_general | solution.py:175
  193.2 5.7 convolution_convert_fusion
  199.3 10.0 multiply_convert_fusion.1
  209.3 9.3 convolution_convert_fusion.1
  222.2 7.4 reduce-scatter.10.cloned.1.call-done
  237.4 11.8 %all-gather.11.cloned.1.call-done = bf16[1024,1024]{1,0:T(8,128)(2,1)} async-done(((bf16[512,1024]{1,0:T(8,128)(2,1)}), bf16[1024,1024]{1,0:T(8,128)(2,1)}) %all-gather.11.cloned.1.call-update) | async-done | bytes 2097168 | tf_op jit(solution)/shard_map/all_gather | solution.py:193
  254.5 103.5 %while.28 = (s32[]{:T(128)}, f32[1024,8,64]{0,2,1:T(8,128)}, f32[1024,8,64]{0,2,1:T(8,128)}, bf16[2,512,8,64]{1,3,2,0:T(8,128)(2,1)}, s32[2]{0:T(128)S(1)}, /*in...) while((s32[]{:T(128)}, f32[1024,8,64]{0,2,1:T(8,128)}, ...), condition=%wide.region_18.19_spmd.clone, body=%wide.region_16.18_spmd.clone.sunk | while | flops 2738352128 | bytes 226628016 | solution.py:230
  262.2 5.7 copy-done.1
  268.0 6.5 bitcast_add_fusion.5
  274.5 12.3 %multiply_reduce_fusion.3 = (f32[8,512]{1,0:T(8,128)S(1)}, f32[8,512,1024]{2,1,0:T(8,128)}) fusion(f32[8,512,1024]{2,1,0:T(8,128)} %copy-done.1, f32[8,512]{1,0:T(8,128)S(1)} %dynamic-slice_bitcast_fusion.2, pred[512,1024]{1,0:T(8,128)(4,1)S(1)} %compare_and_fusion.5, bf16[1024,8,64]{0,2,1:T(8,128)(2,1)} %get-tuple-element.571, ...), kind=kOutput, calls=%fused_computation.14.clone.1 | convolution fusion | flops 553644032 | bytes 35684356 | tf_op jit(solution)/shard_map/while/body/eval_jaxpr/qhe,khe->hqk/dot_general | solution.py:210
  286.8 12.5 %multiply_convert_fusion.4 = bf16[8,512,1024]{2,1,0:T(8,128)(2,1)S(1)} fusion(f32[8,512,1024]{2,1,0:T(8,128)} %get-tuple-element.485, f32[8,512,1024]{2,1,0:T(8,128)} %copy-done.1, f32[8,512]{1,0:T(8,128)S(1)} %get-tuple-element.486, f32[8,512]{1,0:T(8,128)S(1)} %dynamic-slice_bitcast_fusion.2, pred[512,1024]{1,0:T(8,128)(4,1)S(1)} %compare_and_fusion.5), kind=kLoop, calls=%fused_computation.13.clone.1 | loop fusion | flops 20971520 | bytes 42500096 | tf_op jit(solution)/shard_map/while/body/eval_jaxpr/convert_element_type | solution.py:214
  312.6 5.7 copy-done.1
  318.4 6.9 bitcast_add_fusion.5
  325.3 12.3 %multiply_reduce_fusion.3 = (f32[8,512]{1,0:T(8,128)S(1)}, f32[8,512,1024]{2,1,0:T(8,128)}) fusion(f32[8,512,1024]{2,1,0:T(8,128)} %copy-done.1, f32[8,512]{1,0:T(8,128)S(1)} %dynamic-slice_bitcast_fusion.2, pred[512,1024]{1,0:T(8,128)(4,1)S(1)} %compare_and_fusion.5, bf16[1024,8,64]{0,2,1:T(8,128)(2,1)} %get-tuple-element.571, ...), kind=kOutput, calls=%fused_computation.14.clone.1 | convolution fusion | flops 553644032 | bytes 35684356 | tf_op jit(solution)/shard_map/while/body/eval_jaxpr/qhe,khe->hqk/dot_general | solution.py:210
  337.6 12.5 %multiply_convert_fusion.4 = bf16[8,512,1024]{2,1,0:T(8,128)(2,1)S(1)} fusion(f32[8,512,1024]{2,1,0:T(8,128)} %get-tuple-element.485, f32[8,512,1024]{2,1,0:T(8,128)} %copy-done.1, f32[8,512]{1,0:T(8,128)S(1)} %get-tuple-element.486, f32[8,512]{1,0:T(8,128)S(1)} %dynamic-slice_bitcast_fusion.2, pred[512,1024]{1,0:T(8,128)(4,1)S(1)} %compare_and_fusion.5), kind=kLoop, calls=%fused_computation.13.clone.1 | loop fusion | flops 20971520 | bytes 42500096 | tf_op jit(solution)/shard_map/while/body/eval_jaxpr/convert_element_type | solution.py:214
  379.5 6.5 bitcast_convert_fusion
  386.0 8.9 convolution_bitcast_fusion.1
  394.9 9.5 copy.59
  409.4 11.7 %fusion.73 = f32[2048,1024]{0,1:T(8,128)} fusion(bf16[1024,2048]{1,0:T(8,128)(2,1)} %multiply_convert_fusion.1, bf16[1024,1024]{1,0:T(8,128)(2,1)} %all-gather.9.cloned.1.call-done), kind=kOutput, calls=%fused_computation.183 | convolution fusion | flops 4294967296 | bytes 14680064 | tf_op jit(solution)/shard_map/pf,pd->fd/dot_general | solution.py:171
  421.2 10.7 fusion.72
  445.1 45.4 %all-reduce.13 = (f32[1024]{0:T(1024)}, f32[1024]{0:T(1024)}, f32[3,1024]{1,0:T(4,128)}, f32[1024]{0:T(1024)}, f32[1024]{0:T(1024)}, /*index=5*/f32[1024]{0:T(1024)}, f32[4096]{0:T(1024)}, f32[1024]{0:T(1024)}) all-reduce(f32[1024]{0:T(1024)S(1)} %get-tuple-element.228, ...), channel_id=1, replica_groups=mesh['dp'=16,'tensor'=2] {'dp','tensor'}, use_global_device_ids=true, to_apply=%region_23.24 | all-reduce | flops 13312 | bytes 106496 | tf_op jit(solution)/shard_map/psum | solution.py:286
  490.5 172.5 %all-reduce.16.cloned.1.call-done = f32[3,1024,512]{2,0,1:T(4,128)} async-done(((f32[3,1024,512]{2,0,1:T(4,128)}), f32[3,1024,512]{2,0,1:T(4,128)}) %all-reduce.16.cloned.1.call-update) | async-done | bytes 6291472
  665.0 80.3 %reduce-scatter.16.cloned.1.call-done = f32[512,64]{0,1:T(8,128)} async-done(((f32[512,1024]{0,1:T(8,128)}), f32[512,64]{0,1:T(8,128)}) %reduce-scatter.16.cloned.1.call-update) | async-done | bytes 131088 | tf_op jit(solution)/shard_map/reduce_scatter | solution.py:260
  745.3 177.9 %reduce-scatter.20.cloned.1.call-done = f32[2048,64]{0,1:T(8,128)} async-done(((f32[2048,1024]{0,1:T(8,128)}), f32[2048,64]{0,1:T(8,128)}) %reduce-scatter.20.cloned.1.call-update) | async-done | bytes 524304 | tf_op jit(solution)/shard_map/reduce_scatter | solution.py:262
  923.1 183.0 %reduce-scatter.18.cloned.1.call-done = f32[64,2048]{1,0:T(8,128)} async-done(((f32[1024,2048]{1,0:T(8,128)}), f32[64,2048]{1,0:T(8,128)}) %reduce-scatter.18.cloned.1.call-update) | async-done | bytes 524304 | tf_op jit(solution)/shard_map/reduce_scatter | solution.py:261
  (253 shorter events, 151.9 us)
Async XLA Ops:
  7.2 20.7 %copy-start = (bf16[3,1024,512]{2,1,0:T(8,128)(2,1)S(1)}, bf16[3,1024,512]{2,1,0:T(8,128)(2,1)}, u32[]{:S(2)}) copy-start(bf16[3,1024,512]{2,1,0:T(8,128)(2,1)} %param.23) | copy-start | bytes 9437188
  7.2 20.7 %copy-start.52 = (f32[3,512]{1,0:T(4,128)S(1)}, f32[3,512]{1,0:T(4,128)}, u32[]{:S(2)}) copy-start(f32[3,512]{1,0:T(4,128)} %param.24) | copy-start | bytes 18436
  7.2 20.6 %all-gather.5.cloned.1.call-start = ((), (), s32[]{:S(2)}) async-start(), calls=%async_computation.7 | async-start | bytes 3145728 | tf_op jit(solution)/shard_map/all_gather | solution.py:97
  14.4 117.3 %reduce-scatter.8.cloned.1.call-start = ((), (), s32[]{:S(2)}) async-start(), calls=%async_computation.8 | async-start | bytes 3145728 | tf_op jit(solution)/shard_map/reduce_scatter | solution.py:142
  15.2 22.3 %copy-start.27 = (f32[1024,12]{0,1:T(8,128)}, f32[1024,12]{0,1:T(8,128)S(1)}, u32[]{:S(2)}) copy-start(f32[1024,12]{0,1:T(8,128)S(1)} %get-tuple-element.341) | copy-start | bytes 147460
  15.2 22.3 %copy-start.29 = (f32[1024,12]{0,1:T(8,128)}, f32[1024,12]{0,1:T(8,128)S(1)}, u32[]{:S(2)}) copy-start(f32[1024,12]{0,1:T(8,128)S(1)} %get-tuple-element.342) | copy-start | bytes 147460
  15.7 20.1 %copy-start.17 = (f32[1024,10]{0,1:T(8,128)}, f32[1024,10]{0,1:T(8,128)S(1)}, u32[]{:S(2)}) copy-start(f32[1024,10]{0,1:T(8,128)S(1)} %get-tuple-element.337) | copy-start | bytes 122884
  15.7 20.1 %copy-start.19 = (f32[1024,10]{0,1:T(8,128)}, f32[1024,10]{0,1:T(8,128)S(1)}, u32[]{:S(2)}) copy-start(f32[1024,10]{0,1:T(8,128)S(1)} %get-tuple-element.338) | copy-start | bytes 122884
  15.7 20.1 %copy-start.21 = (f32[1024,10]{0,1:T(8,128)}, f32[1024,10]{0,1:T(8,128)S(1)}, u32[]{:S(2)}) copy-start(f32[1024,10]{0,1:T(8,128)S(1)} %get-tuple-element.347) | copy-start | bytes 122884
  15.8 20.1 %copy-start.23 = (f32[1024,10]{0,1:T(8,128)}, f32[1024,10]{0,1:T(8,128)S(1)}, u32[]{:S(2)}) copy-start(f32[1024,10]{0,1:T(8,128)S(1)} %get-tuple-element.348) | copy-start | bytes 122884
  38.9 23.7 %copy-start.26 = (bf16[1024,8,10]{0,2,1:T(8,128)(2,1)S(1)}, bf16[1024,8,10]{0,2,1:T(8,128)(2,1)}, u32[]{:S(2)}) copy-start(bf16[1024,8,10]{0,2,1:T(8,128)(2,1)} %get-tuple-element.310) | copy-start | bytes 491524
  59.8 23.1 %copy-start.31 = (f32[2,8,512]{2,1,0:T(8,128)S(1)}, f32[2,8,512]{2,1,0:T(8,128)}, u32[]{:S(2)}) copy-start(f32[2,8,512]{2,1,0:T(8,128)} %custom-call.2) | copy-start | bytes 98308
  118.1 13.6 %copy-start.32 = (f32[1024]{0:T(1024)S(1)}, f32[1024]{0:T(1024)}, u32[]{:S(2)}) copy-start(f32[1024]{0:T(1024)} %param.26) | copy-start | bytes 12292
  120.7 15.2 %copy-start.36 = (f32[1024]{0:T(1024)S(1)}, f32[1024]{0:T(1024)}, u32[]{:S(2)}) copy-start(f32[1024]{0:T(1024)} %param.27) | copy-start | bytes 12292
  120.7 15.2 %copy-start.48 = (f32[1024]{0:T(1024)S(1)}, f32[1024]{0:T(1024)}, u32[]{:S(2)}) copy-start(f32[1024]{0:T(1024)} %param.28) | copy-start | bytes 12292
  120.7 28.7 %all-gather.7.cloned.1.call-start = ((), (), s32[]{:S(2)}) async-start(), calls=%async_computation.9 | async-start | bytes 3145728 | tf_op jit(solution)/shard_map/all_gather | solution.py:151
  137.5 25.2 %all-gather.9.cloned.1.call-start = ((), (), s32[]{:S(2)}) async-start(), calls=%async_computation.11 | async-start | bytes 3145728 | tf_op jit(solution)/shard_map/all_gather | solution.py:170
  138.1 24.6 %copy-start.46 = (f32[2048]{0:T(1024)S(1)}, f32[2048]{0:T(1024)}, u32[]{:S(2)}) copy-start(f32[2048]{0:T(1024)} %param.30) | copy-start | bytes 24580
  138.1 80.6 %reduce-scatter.12.cloned.1.call-start = ((), (), s32[]{:S(2)}) async-start(), calls=%async_computation.12 | async-start | bytes 3145728 | tf_op jit(solution)/shard_map/reduce_scatter | solution.py:182
  162.7 30.5 %copy-start.50 = (bf16[1024,2048]{1,0:T(8,128)(2,1)S(1)}, bf16[1024,2048]{1,0:T(8,128)(2,1)}, u32[]{:S(2)}) copy-start(bf16[1024,2048]{1,0:T(8,128)(2,1)} %param.29) | copy-start | bytes 12582916
  198.9 30.7 %reduce-scatter.10.cloned.1.call-start = ((), (), s32[]{:S(2)}) async-start(), calls=%async_computation.10 | async-start | bytes 3145728 | tf_op jit(solution)/shard_map/reduce_scatter | solution.py:159
  218.6 11.0 copy-start.49
  218.6 30.6 %all-gather.11.cloned.1.call-start = ((), (), s32[]{:S(2)}) async-start(), calls=%async_computation.13 | async-start | bytes 3145728 | tf_op jit(solution)/shard_map/all_gather | solution.py:193
  237.3 199.3 %reduce-scatter.14.cloned.1.call-start = ((), (), s32[]{:S(2)}) async-start(), calls=%async_computation.14 | async-start | bytes 3145728 | tf_op jit(solution)/shard_map/reduce_scatter | solution.py:248
  286.8 12.5 %copy-start.2 = (bf16[1024,8,64]{0,2,1:T(8,128)(2,1)S(1)}, bf16[1024,8,64]{0,2,1:T(8,128)(2,1)}, u32[]{:S(2)}) copy-start(bf16[1024,8,64]{0,2,1:T(8,128)(2,1)} %get-tuple-element.568) | copy-start | bytes 3145732 | tf_op jit(solution)/shard_map/while
  286.8 12.5 %copy-start.13 = (bf16[2,512,8,64]{1,3,2,0:T(8,128)(2,1)S(1)}, bf16[2,512,8,64]{1,3,2,0:T(8,128)(2,1)}, u32[]{:S(2)}) copy-start(bf16[2,512,8,64]{1,3,2,0:T(8,128)(2,1)} %get-tuple-element.546) | copy-start | bytes 3145732 | tf_op jit(solution)/shard_map/while
  337.6 12.5 %copy-start.2 = (bf16[1024,8,64]{0,2,1:T(8,128)(2,1)S(1)}, bf16[1024,8,64]{0,2,1:T(8,128)(2,1)}, u32[]{:S(2)}) copy-start(bf16[1024,8,64]{0,2,1:T(8,128)(2,1)} %get-tuple-element.568) | copy-start | bytes 3145732 | tf_op jit(solution)/shard_map/while
  337.6 12.5 %copy-start.13 = (bf16[2,512,8,64]{1,3,2,0:T(8,128)(2,1)S(1)}, bf16[2,512,8,64]{1,3,2,0:T(8,128)(2,1)}, u32[]{:S(2)}) copy-start(bf16[2,512,8,64]{1,3,2,0:T(8,128)(2,1)} %get-tuple-element.546) | copy-start | bytes 3145732 | tf_op jit(solution)/shard_map/while
  386.0 277.0 %all-reduce.16.cloned.1.call-start = ((), (), s32[]{:S(2)}) async-start(), calls=%async_computation.18 | async-start | bytes 16777216
  404.4 340.9 %reduce-scatter.16.cloned.1.call-start = ((), (), s32[]{:S(2)}) async-start(), calls=%async_computation.15 | async-start | bytes 2228224 | tf_op jit(solution)/shard_map/reduce_scatter | solution.py:260
  409.1 514.0 %reduce-scatter.20.cloned.1.call-start = ((), (), s32[]{:S(2)}) async-start(), calls=%async_computation.17 | async-start | bytes 8912896 | tf_op jit(solution)/shard_map/reduce_scatter | solution.py:262
  421.1 685.0 %reduce-scatter.18.cloned.1.call-start = ((), (), s32[]{:S(2)}) async-start(), calls=%async_computation.16 | async-start | bytes 8912896 | tf_op jit(solution)/shard_map/reduce_scatter | solution.py:261
  (44 other events, 152.1 us)
Sparse Core Ops, SparseCore 0:
  14.5 13.3 all-gather.4
  120.8 10.7 reduce-scatter.7
  137.6 11.7 all-gather.6
  150.9 11.7 all-gather.8
  199.0 10.7 reduce-scatter.11
  218.8 10.7 reduce-scatter.9
  237.4 11.7 all-gather.10
  386.1 10.7 reduce-scatter.13
  404.6 258.4 all-reduce.15
  665.7 79.5 reduce-scatter.15
  748.2 174.9 reduce-scatter.19
  925.9 180.2 reduce-scatter.17
where the time goes:
time: 1120 us; the launch traced here: 1110 us
  waiting for transfers between devices  670 us (60%)
  matrix products  186 us (17%)
  other arithmetic  97.8 us (9%)
  local copies, waits for them, and re-layouts  90.2 us (8%)
  blocking collectives  45.4 us (4%)
  between operations  15.9 us (1%)
    reduce_scatter x1, waiting for transfers between devices, on_device(): lax.psum_scatter(grad_up_weight, 'dp', scatter_dimension=0, tiled=True)  183 us
    reduce_scatter x1, waiting for transfers between devices, on_device(): lax.psum_scatter(grad_down_weight, 'dp', scatter_dimension=1, tiled=True)  178 us
    unnamed x13, waiting for transfers between devices  173 us
    reduce_scatter x1, waiting for transfers between devices, on_device(): lax.psum_scatter(grad_out_weight, 'dp', scatter_dimension=1, tiled=True)  80.3 us
    psum x1, blocking collectives, on_device(): lax.psum((grad_attn_gain, grad_attn_shift, full_proj_bias, grad_out_bias,...  45.4 us
    concatenate x2, local copies, waits for them, and re-layouts, rotate(): return jnp.concatenate(pieces, axis=-1)  40 us
    dot_general x1, matrix products, on_device(): jnp.einsum('pd,fd->pf', cot_full, down_weight, preferred_element_type=jnp...  28.4 us
    convert_element_type x2, other arithmetic, backward_block(): grad_scores = (attention * (grad_attention - inner)).astype(jnp.bfloat16)  25 us
  transfers between devices with their start and end apart: 12, of which 10 were waited for; matrix products, arithmetic and copies ran while one was open for 8% of the time, Pallas kernels for 0%

commit v1 on v0

v1 whole, which is shorter than its diff:
```python
import functools
import math

import jax
import jax.numpy as jnp
import ml_dtypes
import numpy as np
from jax import lax
from jax.experimental import pallas as pl
from jax.experimental.pallas import tpu as pltpu
from jax.sharding import PartitionSpec as P

HEAD = 64
GRID = 16
FRAME = 258
EPS = 1e-6
LANES = 128
FC = 256
MESH = pl.DeviceIdType.MESH
F32 = jnp.float32
BF = jnp.bfloat16
NEG = -1e30
FRAMES = 4
TERM = 16


def nn(a, b):
    return jnp.dot(a, b, preferred_element_type=F32)


def nt(a, b):
    return lax.dot_general(a, b, (((1,), (1,)), ((), ())), preferred_element_type=F32)


def rope_tables():
    side = 2 * (HEAD // 6)
    sections = (HEAD - 2 * side, side, side)
    cos = np.zeros((FRAMES + 2 * GRID, HEAD), np.float64)
    sin = np.zeros((FRAMES + 2 * GRID, HEAD), np.float64)
    lane, row = 0, 0
    for width, count in zip(sections, (FRAMES, GRID, GRID)):
        half = width // 2
        freq = np.float32(10000.0) ** (-np.arange(half, dtype=np.float32) * np.float32(2.0) / np.float32(width))
        angle = (np.arange(count, dtype=np.float32)[:, None] * freq.astype(np.float32)[None, :]).astype(np.float64)
        cos[row : row + count, lane : lane + half] = np.cos(angle)
        cos[row : row + count, lane + half : lane + width] = np.cos(angle)
        sin[row : row + count, lane : lane + half] = -np.sin(angle)
        sin[row : row + count, lane + half : lane + width] = np.sin(angle)
        lane, row = lane + width, row + count
    both = np.concatenate([cos, cos, sin, sin], axis=1).astype(np.float32)
    out = np.zeros((LANES, 4 * HEAD), ml_dtypes.bfloat16)
    rest, n = both, both.shape[0]
    for term in range(3):
        part = rest.astype(ml_dtypes.bfloat16)
        out[term * n : (term + 1) * n] = part
        rest = rest - part.astype(np.float32)
    return out


def partner_of(x, lane):
    side = 2 * (HEAD // 6)
    first = HEAD - 2 * side
    a, b = first // 2, side // 2
    within = lane % HEAD
    past = (within - first) % side
    up_a = pltpu.roll(x, LANES - a, 1)
    down_a = pltpu.roll(x, a, 1)
    up_b = pltpu.roll(x, LANES - b, 1)
    down_b = pltpu.roll(x, b, 1)
    in_first = jnp.where(within < a, up_a, down_a)
    in_side = jnp.where(past < b, up_b, down_b)
    return jnp.where(within < first, in_first, in_side)


def split3(x):
    hi = x.astype(BF).astype(F32)
    mid = (x - hi).astype(BF).astype(F32)
    return hi, mid, x - hi - mid


def kernel(
    dp, tok_h, cot_h, pw_h, ow_h, uw_h, dw_h, lens, gain1, shift1, pbias, obias, gain2, shift2, ubias, dbias, table,
    mixed_h, gtok_h, gout, small, U, DN, OW, TOKX, N1, T1, T2, CG, N2, QA, K, V, ATT, ACT, GH, MID, X1, S1,
    ONE, QF, KF, SB, SBR, G, *rest,
):
    stages = dp.bit_length() - 1
    RM, RP = rest[:stages], rest[stages : 2 * stages]
    m_send, m_recv, p_send, p_recv, x_send, x_recv, b_send, b_recv, loads = rest[2 * stages :]
    T = tok_h.shape[0]
    D = tok_h.shape[1]
    R = 2 * T
    E = OW.shape[0]
    F = DN.shape[0]
    pairs = E // LANES
    nf = F // FC
    low = stages - 4
    unit = 1 << low
    me = lax.axis_index("dp")
    core = lax.axis_index("tensor")
    lane = lax.broadcasted_iota(jnp.int32, (1, LANES), 1)

    def bit_of(stride):
        return (me // stride) % 2

    def partner(stride):
        return me + (1 - 2 * bit_of(stride)) * stride

    def load(src, dst, k):
        return pltpu.make_async_copy(src, dst, loads.at[k])

    tok_load = load(tok_h, TOKX, 0)
    cot_load = load(cot_h, CG.at[pl.ds(0, T)], 1)
    pw_loads = [load(pw_h.at[c], U.at[:, pl.ds(c * E, E)], 2 + c) for c in range(3)]
    ow_load = load(ow_h, OW, 5)
    uw_load = load(uw_h, U, 6)
    dw_load = load(dw_h, DN, 7)
    pw_again = [load(pw_h.at[c], U.at[:, pl.ds(c * E, E)], 8 + c) for c in range(3)]
    tok_again = load(tok_h, N2.at[pl.ds(0, T)], 11)
    mixed_store = load(N2.at[pl.ds(0, T)], mixed_h, 12)
    gtok_store = load(MID, gtok_h, 13)
    tok_load.start()
    cot_load.start()
    for c in pw_loads:
        c.start()
    ow_load.start()
    dw_load.start()

    barrier = pltpu.get_barrier_semaphore()
    peers = [(partner(1 << b), core) for b in range(stages)] + [(me, 1 - core)]
    for who in peers:
        pl.semaphore_signal(barrier, inc=1, device_id=who, device_id_type=MESH)
    pl.semaphore_wait(barrier, len(peers))

    def cross(src, dst, k):
        return pltpu.make_async_remote_copy(
            src_ref=src, dst_ref=dst, send_sem=x_send.at[k], recv_sem=x_recv.at[k],
            device_id=(me, 1 - core), device_id_type=MESH,
        )

    half = T // 2

    def turned(dst, src, first, count):
        @pl.loop(first // 256, (first + count) // 256)
        def _(m):
            rows = pl.ds(pl.multiple_of(m * 256, 256), 256)
            dst[:, rows] = src[rows].T

    def cross_rows(src, s0, dst, d0, base, m):
        return cross(src.at[pl.ds(s0 + m * half, half)], dst.at[pl.ds(d0 + m * half, half)], base + m)

    def order_of(kind, par):
        where = {"x": unit * (1 + par), "y": unit * (2 - par), "z": unit * 4, "Z": unit * 8}
        return [where[k] for k in kind + "Z"] + [1 << b for b in reversed(range(low))]

    def places_of(kind, par):
        w = {k: 8 >> i for i, k in enumerate(kind + "Z")}
        return (w["x"] + par * (w["y"] - w["x"]), w["y"] + par * (w["x"] - w["y"]), w["z"], w["Z"])

    def g_view(fam, c):
        if fam == "M":
            return G.at[c % 8]
        if fam == "O":
            return G.at[8 + c]
        p, k = c
        return G.at[p + 4 * (k // 2), :, pl.ds((k % 2) * LANES, LANES)]

    def slot(fam, c):
        if fam == "M":
            return RM, c, m_send, m_recv
        if fam == "O":
            return RM, 2 * nf + c, m_send, m_recv
        return RP, 3 * c[0] + c[1], p_send, p_recv

    block = D // 16

    def put(fam, c, value, row0, kind, par):
        w = places_of(kind, par)
        view = g_view(fam, c)
        for b in range(value.shape[0] // block):
            n = row0 * (value.shape[0] // block) + b
            place = ((n % 2) * w[0] + ((n // 2) % 2) * w[1] + ((n // 4) % 2) * w[2] + (n // 8) * w[3]) * block
            view[pl.ds(pl.multiple_of(place, block), block), :] = value[b * block : (b + 1) * block].astype(BF)

    def rs_parts(fam, c, s, order):
        R_, at, ss, rr = slot(fam, c)
        view = g_view(fam, c) if s == 0 else R_[s - 1].at[at]
        n = D >> s
        h = n // 2
        bit = bit_of(order[s])
        if h >= 16:
            src = view.at[pl.ds(pl.multiple_of((1 - bit) * h, 16), h)]
            keep = view.at[pl.ds(pl.multiple_of(bit * h, 16), h)]
        else:
            src = keep = view
        copy = pltpu.make_async_remote_copy(
            src_ref=src, dst_ref=R_[s].at[at], send_sem=ss.at[at, s], recv_sem=rr.at[at, s],
            device_id=(partner(order[s]), core), device_id_type=MESH,
        )
        return copy, keep, R_[s].at[at], bit, h

    def columns_of(fam, c):
        if fam == "M":
            return pl.multiple_of((c % 2) * F + (c // 2) * FC, FC), FC
        if fam == "O":
            return 2 * F + c * FC, FC
        return pl.multiple_of(2 * F + E + c[1] * E + c[0] * LANES, LANES), LANES

    def rs_start(fam, c, s, order):
        rs_parts(fam, c, s, order)[0].start()

    def rs_step(fam, c, s, order):
        copy, keep, landed, bit, h = rs_parts(fam, c, s, order)
        copy.wait()
        if s < stages - 1:
            n = landed.shape[0]
            piece = min(n, 64)
            if n == piece:
                landed[...] = landed[...] + keep[...]
            else:
                @pl.loop(0, n // piece)
                def _(q):
                    at = pl.ds(pl.multiple_of(q * piece, piece), piece)
                    landed[at] = landed[at] + keep[at]

            rs_start(fam, c, s + 1, order)
        else:
            total = landed[...].astype(F32) + keep[...].astype(F32)
            if h < 16:
                total = jnp.where(bit == 1, total[8:], total[:8])
            start, width = columns_of(fam, c)
            gout[:, pl.ds(start, width)] = total

    M_KINDS = ("xyz", "yzx", "zxy", "yxz")

    def m_kind(e, k):
        return M_KINDS[2 * e + k]

    def m_par(i):
        return (i // 2) % 2

    def m_steps(i, e, s):
        for k in range(2):
            rs_step("M", 2 * i + k, s, order_of(m_kind(e, k), m_par(i)))

    O_KINDS = ("xzy", "zyx")
    P_KINDS = ("xyz", "yzx", "zxy")

    def normed(x):
        centre = x - jnp.mean(x, axis=1, keepdims=True)
        inv = lax.rsqrt(jnp.mean(centre * centre, axis=1, keepdims=True) + EPS)
        return centre * inv, inv

    tok_load.wait()

    @pl.loop(0, 2)
    def _(m):
        @pl.loop(0, half // 128)
        def _(q):
            rows = pl.ds(m * half + q * 128, 128)
            x = TOKX[rows].astype(F32)
            N1[rows] = (normed(x)[0] * gain1[...] + shift1[...]).astype(BF)

        cross_rows(N1, 0, N1, T, 1, m).start()

    cot_load.wait()
    cot_send = cross(CG.at[pl.ds(0, T)], CG.at[pl.ds(T, T)], 0)
    cot_send.start()

    @pl.loop(0, R // 256)
    def _(m):
        row = lax.broadcasted_iota(jnp.int32, (256, 1), 0) + m * 256
        place = (row + core * T) % R
        begin = jnp.zeros((256, 1), jnp.int32)
        episode = jnp.zeros((256, 1), jnp.int32)
        end = jnp.int32(0)
        for e in range(lens.shape[1] - 1):
            end = end + lens[0, e]
            begin = jnp.where(place >= end, end, begin)
            episode = jnp.where(place >= end, e + 1, episode)
        local = place - begin
        frame = jnp.zeros((256, 1), jnp.int32)
        for k in range(1, FRAMES):
            frame = jnp.where(local >= k * FRAME, k, frame)
        inside = local - frame * FRAME
        patch = jnp.maximum(inside - 2, 0)
        row_pos = jnp.where(inside >= 2, patch // GRID, 0)
        col_pos = jnp.where(inside >= 2, patch % GRID, 0)
        n = FRAMES + 2 * GRID
        spot = lane % n
        hit = (spot == frame) | (spot == FRAMES + row_pos) | (spot == FRAMES + GRID + col_pos)
        hit = hit & (lane < 3 * n)
        rows = pl.ds(m * 256, 256)
        ONE[rows] = jnp.where(hit, 1.0, 0.0).astype(BF)
        feature = lane % HEAD
        counted = (feature // FRAMES == episode) & (feature % FRAMES <= frame)
        is_class = feature < TERM
        QF[rows] = jnp.where(is_class & jnp.logical_not(counted), NEG, 0.0).astype(BF)
        ones = (feature == episode * FRAMES + frame) | ((feature >= TERM) & (feature < TERM + 3))
        KF[rows] = jnp.where(ones, 1.0, 0.0).astype(BF)

    def rotary(rows):
        both = nn(ONE[rows], table[...])
        return both[:, :LANES], both[:, LANES:]

    for c in pw_loads:
        c.wait()

    def project(m):
        rows = pl.ds(m * 256, 256)
        x = N1[rows]
        cos, sin = rotary(rows)
        q = nn(x, U[:, 0:E]) + pbias[:, 0:E]
        for p in range(pairs):
            v = q[:, p * LANES : (p + 1) * LANES]
            v = ((v * cos + partner_of(v, lane) * sin) * HEAD**-0.5).astype(BF)
            QA[2 * p, rows] = jnp.where(lane < HEAD, v, QF[rows])
            QA[2 * p + 1, rows] = jnp.where(lane >= HEAD, v, QF[rows])
        k = nn(x, U[:, E : 2 * E]) + pbias[:, E : 2 * E]
        for p in range(pairs):
            v = k[:, p * LANES : (p + 1) * LANES]
            K[rows, p * LANES : (p + 1) * LANES] = (v * cos + partner_of(v, lane) * sin).astype(BF)
        V[rows] = (nn(x, U[:, 2 * E : 3 * E]) + pbias[:, 2 * E : 3 * E]).astype(BF)

    @pl.loop(0, 2)
    def _(m):
        project(m)

    turned(T1, CG, 0, T)

    @pl.loop(0, 2)
    def _(m):
        cross_rows(N1, 0, N1, T, 1, m).wait()
        project(2 + m)

    uw_load.start()

    def mine(e):
        return lane < HEAD if e == 0 else lane >= HEAD

    def key_sets(p, box):
        cols = pl.ds(pl.multiple_of(p * LANES, LANES), LANES)
        for e in range(2):
            box[:, e * LANES : (e + 1) * LANES] = jnp.where(mine(e), K[:, cols], KF[...])
            box[:, (2 + e) * LANES : (3 + e) * LANES] = jnp.where(mine(e), V[:, cols], jnp.ones((), BF))

    def attend(first):
        @pl.loop(0, pairs)
        def _(p):
            key_sets(p, T2)

            @pl.loop(0, T // 256)
            def _(b):
                rows = pl.ds(first + b * 256, 256)
                parts = []
                for e in range(2):
                    qa = QA[2 * p + e, rows]
                    s = nt(qa, T2[:, e * LANES : (e + 1) * LANES])
                    top = jnp.max(s, axis=1, keepdims=True)
                    w = jnp.exp(s - top).astype(BF)
                    o = nn(w, T2[:, (2 + e) * LANES : (3 + e) * LANES])
                    parts.append(o / pltpu.roll(o, HEAD, 1))
                    total = jnp.where(mine(e), 1.0, o)
                    hi, mid, lo = split3(top + jnp.log(total))
                    feature = lane % HEAD
                    terms = jnp.where(feature == TERM, -hi, jnp.where(feature == TERM + 1, -mid, -lo)).astype(BF)
                    is_term = (feature >= TERM) & (feature < TERM + 3) & jnp.logical_not(mine(e))
                    QA[2 * p + e, rows] = jnp.where(is_term, terms, qa)
                ATT[rows, pl.ds(pl.multiple_of(p * LANES, LANES), LANES)] = jnp.where(
                    lane < HEAD, parts[0], parts[1]
                ).astype(BF)

    attend(T)
    ow_load.wait()

    @pl.loop(0, 2)
    def _(m):
        rows = pl.ds(m * half, half)
        S1[rows] = nn(ATT[pl.ds(T + m * half, half)], OW[...]).astype(BF)
        cross_rows(S1, 0, X1, 0, 3, m).start()

    attend(0)

    @pl.loop(0, 2)
    def _(m):
        rows = pl.ds(m * half, half)
        MID[rows] = nn(ATT[rows], OW[...])
        cross_rows(S1, 0, X1, 0, 3, m).wait()

        @pl.loop(0, half // 128)
        def _(q):
            rows = pl.ds(m * half + q * 128, 128)
            mid = TOKX[rows].astype(F32) + (MID[rows] + X1[rows].astype(F32) + obias[...])
            MID[rows] = mid
            N2[rows] = (normed(mid)[0] * gain2[...] + shift2[...]).astype(BF)

        cross_rows(N2, 0, N2, T, 5, m).start()

    SB[...] = jnp.zeros_like(SB)
    SB[12:13] = jnp.sum(CG[0:T].astype(F32), axis=0, keepdims=True)
    turned(T2, N2, 0, T)
    cot_send.wait()
    turned(T1, CG, T, T)

    @pl.loop(0, 2)
    def _(m):
        cross_rows(N2, 0, N2, T, 5, m).wait()

    turned(T2, N2, T, T)
    uw_load.wait()
    dw_load.wait()

    ones8 = jnp.ones((8, R), BF)

    def hidden_chunk(i, e):
        cols = pl.ds(pl.multiple_of(i * FC, FC), FC)

        @pl.loop(0, R // 256)
        def _(m):
            rows = pl.ds(m * 256, 256)
            h = nn(N2[rows], U[:, cols]) + ubias[:, cols]
            cdf = 0.5 + 0.5 * lax.erf(h * math.sqrt(0.5))
            ACT[rows, cols] = (h * cdf).astype(BF)
            slope = cdf + h * jnp.exp(h * h * -0.5) * (1.0 / math.sqrt(2 * math.pi))
            GH[rows, cols] = (nt(CG[rows], DN[cols]) * slope).astype(BF)

        for k, (left, right) in enumerate(((T1, ACT), (T2, GH))):
            @pl.loop(0, D // 256)
            def _(m):
                put("M", 2 * i + k, nn(left[pl.ds(m * 256, 256)], right[:, cols]), m, m_kind(e, k), m_par(i))

            rs_start("M", 2 * i + k, 0, order_of(m_kind(e, k), m_par(i)))

        sums = nn(ones8, GH[:, cols])
        per = D // FC
        SB[pl.ds(8 + core * (F // D) + i // per, 1), pl.ds(pl.multiple_of((i % per) * FC, FC), FC)] = sums[0:1]

    @pl.loop(0, nf // 2)
    def _(j):
        for e in range(2):
            i = 2 * j + e
            hidden_chunk(i, e)
            for s in range(stages):
                lag = LAGS[s]
                if lag < nf:
                    @pl.when(i >= lag)
                    def _():
                        m_steps(i - lag, (e - lag) % 2, s)

    left = [(i + LAGS[s], -s, i, s) for s in range(stages) for i in range(nf) if i + LAGS[s] >= nf]
    left = [(i, s) for _, _, i, s in sorted(left)]

    def drain(count):
        for _ in range(min(count, len(left))):
            i, s = left.pop(0)
            m_steps(i, i % 2, s)

    def norm_back(g, x, gain, row):
        xhat, inv = normed(x)
        SB[row : row + 1] += jnp.sum(g * xhat, axis=0, keepdims=True)
        SB[row + 1 : row + 2] += jnp.sum(g, axis=0, keepdims=True)
        gx = g * gain
        a = jnp.mean(gx, axis=1, keepdims=True)
        b = jnp.mean(gx * xhat, axis=1, keepdims=True)
        return inv * (gx - a - xhat * b)

    @pl.loop(0, 2)
    def _(m):
        S1[pl.ds(m * half, half)] = nt(GH[pl.ds(T + m * half, half)], U[...]).astype(BF)
        cross_rows(S1, 0, X1, 0, 7, m).start()

    drain(DRAIN[0])

    @pl.loop(0, 2)
    def _(m):
        rows = pl.ds(m * half, half)
        own = nt(GH[rows], U[...])
        cross_rows(S1, 0, X1, 0, 7, m).wait()
        for q in range(half // 128):
            at = pl.ds(m * half + q * 128, 128)
            g = own[q * 128 : (q + 1) * 128] + X1[at].astype(F32)
            total = CG[at].astype(F32) + norm_back(g, MID[at], gain2[...], 6)
            high = total.astype(BF)
            CG[at] = high
            TOKX[at] = (total - high.astype(F32)).astype(BF)
            SB[5:6] += jnp.sum(high.astype(F32), axis=0, keepdims=True)
        cross_rows(CG, 0, CG, T, 9, m).start()

    for c in pw_again:
        c.start()

    @pl.loop(0, 2)
    def _(m):
        S1[pl.ds(m * half, half)] = nn(ACT[pl.ds(T + m * half, half)], DN[...]).astype(BF)
        cross_rows(S1, 0, N2, T, 11, m).start()

    drain(DRAIN[1])

    def grad_attended(m):
        rows = pl.ds(m * half, half)
        GH[rows, 0:E] = nt(CG[rows], OW[...]).astype(BF)

    @pl.loop(0, 2)
    def _(m):
        grad_attended(m)

    turned(T1, CG, 0, T)

    @pl.loop(0, 2)
    def _(m):
        cross_rows(CG, 0, CG, T, 9, m).wait()
        grad_attended(2 + m)

    turned(T1, CG, T, T)
    for c in range(2):
        @pl.loop(0, D // 256)
        def _(m):
            put("O", c, nn(T1[pl.ds(m * 256, 256)], ATT[:, c * FC : (c + 1) * FC]), m, O_KINDS[c], 0)

        rs_start("O", c, 0, order_of(O_KINDS[c], 0))
    drain(DRAIN[2])
    turned(T2, N1, 0, R)

    @pl.loop(0, 2)
    def _(m):
        rows = pl.ds(m * half, half)
        own = nn(ACT[rows], DN[...])
        cross_rows(S1, 0, N2, T, 11, m).wait()
        N2[rows] = (MID[rows] + (own + N2[pl.ds(T + m * half, half)].astype(F32) + dbias[...])).astype(BF)

    mixed_store.start()
    drain(DRAIN[3])

    def p_step(p, s):
        for k in range(3):
            rs_step("P", (p, k), s, order_of(P_KINDS[k], 0))

    def o_step(s):
        for c in range(2):
            rs_step("O", c, s, order_of(O_KINDS[c], 0))

    def pair_grads(b):
        rows = pl.ds((b % 2) * 256, 256)
        return [(rows, pl.ds(pl.multiple_of((b // 2) * 2 * LANES + k * LANES, LANES), LANES)) for k in range(2)]

    def query_grads(a, e):
        return pl.ds(a * LANES + e * HEAD, HEAD), pl.ds(D // 2, T)

    plan = []
    for _ in range(pairs):
        mine_now = left[: DRAIN[4]]
        del left[: DRAIN[4]]
        plan.append(mine_now)

    @pl.loop(0, pairs)
    def _(p):
        cols = pl.ds(pl.multiple_of(p * LANES, LANES), LANES)
        key_sets(p, T1)
        N1[0:LANES] = K[:, cols].T
        for e in range(2):
            @pl.loop(0, R // 256)
            def _(b):
                rows = pl.ds(b * 256, 256)
                g = GH[rows, cols]
                both = g.astype(F32) * ATT[rows, cols].astype(F32)
                inner = jnp.sum(jnp.where(mine(e), both, 0.0), axis=1, keepdims=True)
                hi, mid, lo = split3(inner)
                feature = lane % HEAD
                terms = jnp.where(feature == TERM, -hi, jnp.where(feature == TERM + 1, -mid, -lo))
                is_term = (feature >= TERM) & (feature < TERM + 3)
                terms = jnp.where(is_term, terms, 0.0).astype(BF)
                T1[rows, (4 + e) * LANES : (5 + e) * LANES] = jnp.where(mine(e), g, terms)

        for e in range(2):
            for a in range(2):
                MID[query_grads(a, e)] = jnp.zeros((HEAD, T), F32)

            @pl.loop(0, R // 256)
            def _(b):
                rows = pl.ds(b * 256, 256)
                dk = dv = 0.0
                for a in range(2):
                    across = pl.ds(a * T, T)
                    qa = QA[2 * p + e, across]
                    ga = T1[across, (4 + e) * LANES : (5 + e) * LANES]
                    w = jnp.exp(nt(T1[rows, e * LANES : (e + 1) * LANES], qa))
                    ds = (w * nt(T1[rows, (2 + e) * LANES : (3 + e) * LANES], ga)).astype(BF)
                    dv += nn(w.astype(BF), ga)
                    dk += nn(ds, qa)
                    MID[query_grads(a, e)] += nn(N1[e * HEAD : (e + 1) * HEAD, rows], ds)
                for at, g in zip(pair_grads(b), (dk, dv)):
                    MID[at] = g if e == 0 else jnp.where(mine(1), g, MID[at])

            for q, todo in enumerate(plan):
                here = todo[len(todo) // 2 :] if e else todo[: len(todo) // 2]
                if here:
                    @pl.when(p == q)
                    def _():
                        for i, s in here:
                            m_steps(i, i % 2, s)

        @pl.loop(0, R // 256)
        def _(b):
            rows = pl.ds(b * 256, 256)
            cos, sin = rotary(rows)
            turn = MID[pl.ds((b // 2) * LANES, LANES), pl.ds(pl.multiple_of(D // 2 + (b % 2) * 256, 256), 256)]

            def back(g):
                g = g.astype(BF).astype(F32)
                return g * cos - partner_of(g, lane) * sin

            parts = (
                back(turn.T) * HEAD**-0.5,
                *(f(MID[at]) for f, at in zip((back, lambda g: g), pair_grads(b))),
            )
            for c, part in enumerate(parts):
                GH[rows, pl.ds(pl.multiple_of(E + c * E + p * LANES, LANES), LANES)] = part.astype(BF)

        for c in range(3):
            own_cols = pl.ds(pl.multiple_of(E + c * E + p * LANES, LANES), LANES)
            at = core * E + p * LANES
            SB[2 + c : 3 + c, pl.ds(pl.multiple_of(at, LANES), LANES)] = nn(ones8, GH[:, own_cols])[0:1]

            @pl.loop(0, D // 256)
            def _(m):
                put("P", (p, c), nn(T2[pl.ds(m * 256, 256)], GH[:, own_cols]), m, P_KINDS[c], 0)

            rs_start("P", (p, c), 0, order_of(P_KINDS[c], 0))

        for s in range(stages):
            if s + 1 < pairs:
                @pl.when(p == s + 1)
                def _():
                    o_step(s)

            if P_LAGS[s] < pairs:
                @pl.when(p >= P_LAGS[s])
                def _():
                    p_step(p - P_LAGS[s], s)

    for c in pw_again:
        c.wait()
    mixed_store.wait()
    tok_again.start()

    @pl.loop(0, 2)
    def _(m):
        S1[pl.ds(m * half, half)] = nt(GH[pl.ds(T + m * half, half), E : 4 * E], U[:, : 3 * E]).astype(BF)
        cross_rows(S1, 0, X1, 0, 13, m).start()

    drain(len(left))
    tok_again.wait()

    @pl.loop(0, 2)
    def _(m):
        rows = pl.ds(m * half, half)
        own = nt(GH[rows, E : 4 * E], U[:, : 3 * E])
        cross_rows(S1, 0, X1, 0, 13, m).wait()
        for q in range(half // 128):
            at = pl.ds(m * half + q * 128, 128)
            g = own[q * 128 : (q + 1) * 128] + X1[at].astype(F32)
            before = CG[at].astype(F32) + TOKX[at].astype(F32)
            MID[at] = before + norm_back(g, N2[at].astype(F32), gain1[...], 0)

    gtok_store.start()

    later = [(s + 1, s, "O", 0) for s in range(stages) if s + 1 >= pairs]
    later += [(p + P_LAGS[s], s, "P", p) for s in range(stages) for p in range(pairs) if p + P_LAGS[s] >= pairs]
    later.sort(key=lambda z: (z[0], -z[1]))
    per = -(-len(later) // (stages + 1))

    def sums(s):
        who = (partner(1 << s), core) if s < stages else (me, 1 - core)
        return pltpu.make_async_remote_copy(
            src_ref=SB, dst_ref=SBR.at[s], send_sem=b_send.at[s], recv_sem=b_recv.at[s],
            device_id=who, device_id_type=MESH,
        )

    for s in range(stages + 1):
        sums(s).start()
        for _, st, fam, p in later[s * per : (s + 1) * per]:
            if fam == "O":
                o_step(st)
            else:
                p_step(p, st)
        sums(s).wait()
        SB[...] = SB[...] + SBR[s]
    small[...] = SB[...]
    gtok_store.wait()


LAGS = (1, 2, 3, 4, 5, 6, 7)
P_LAGS = (1, 2, 3, 4, 5, 6, 7)
DRAIN = (1, 2, 2, 1, 3)


def on_device(
    tokens, episode_lengths, attn_gain, attn_shift, proj_weight, proj_bias, out_weight, out_bias,
    mlp_gain, mlp_shift, up_weight, up_bias, down_weight, down_bias, cotangent,
):
    dp = lax.axis_size("dp")
    stages = dp.bit_length() - 1
    T, D = tokens.shape
    R = 2 * T
    E = proj_weight.shape[2]
    F = up_weight.shape[1]
    pairs = E // LANES
    nf = F // FC
    columns = 2 * F + 4 * E
    row = lambda v: v.reshape(1, -1).astype(F32)
    rows_at = [max(D >> (s + 1), 16) for s in range(stages)]
    vmem = pl.BlockSpec(memory_space=pltpu.VMEM)
    hbm = pl.BlockSpec(memory_space=pl.ANY)
    smem = pl.BlockSpec(memory_space=pltpu.SMEM)
    dma = pltpu.SemaphoreType.DMA
    scratch = [
        pltpu.VMEM((D, F), BF),
        pltpu.VMEM((F, D), BF),
        pltpu.VMEM((E, D), BF),
        pltpu.VMEM((T, D), BF),
        pltpu.VMEM((R, D), BF),
        pltpu.VMEM((D, R), BF),
        pltpu.VMEM((D, R), BF),
        pltpu.VMEM((R, D), BF),
        pltpu.VMEM((R, D), BF),
        pltpu.VMEM((2 * pairs, R, LANES), BF),
        pltpu.VMEM((R, E), BF),
        pltpu.VMEM((R, E), BF),
        pltpu.VMEM((R, E), BF),
        pltpu.VMEM((R, F), BF),
        pltpu.VMEM((R, F), BF),
        pltpu.VMEM((T, D), F32),
        pltpu.VMEM((T, D), BF),
        pltpu.VMEM((T, D), BF),
        pltpu.VMEM((R, LANES), BF),
        pltpu.VMEM((R, LANES), BF),
        pltpu.VMEM((R, LANES), BF),
        pltpu.VMEM((16, D), F32),
        pltpu.VMEM((stages + 1, 16, D), F32),
        pltpu.VMEM((10, D, FC), BF),
        *[pltpu.VMEM((2 * nf + 2, n, FC), BF) for n in rows_at],
        *[pltpu.VMEM((3 * pairs, n, LANES), BF) for n in rows_at],
        dma((2 * nf + 2, stages)), dma((2 * nf + 2, stages)),
        dma((3 * pairs, stages)), dma((3 * pairs, stages)),
        dma((15,)), dma((15,)), dma((stages + 1,)), dma((stages + 1,)), dma((14,)),
    ]
    mixed, grad_tokens, shard, small = pl.pallas_call(
        functools.partial(kernel, dp),
        out_shape=(
            jax.ShapeDtypeStruct((T, D), BF),
            jax.ShapeDtypeStruct((T, D), F32),
            jax.ShapeDtypeStruct((D // dp, columns), F32),
            jax.ShapeDtypeStruct((16, D), F32),
        ),
        in_specs=[hbm] * 6 + [smem] + [vmem] * 9,
        out_specs=(hbm, hbm, vmem, vmem),
        scratch_shapes=scratch,
        compiler_params=pltpu.CompilerParams(
            collective_id=0, has_side_effects=True, vmem_limit_bytes=63 << 20
        ),
        name="block",
    )(
        tokens, cotangent, proj_weight, out_weight, up_weight, down_weight, episode_lengths,
        row(attn_gain), row(attn_shift), row(proj_bias), row(out_bias), row(mlp_gain), row(mlp_shift),
        row(up_bias), row(down_bias), jnp.asarray(rope_tables()),
    )
    down = shard[:, :F].T
    up = shard[:, F : 2 * F]
    out = shard[:, 2 * F : 2 * F + E].T
    proj = jnp.stack([shard[:, 2 * F + (1 + c) * E : 2 * F + (2 + c) * E] for c in range(3)])
    return (
        mixed, grad_tokens, small[0], small[1], proj, small[2:5], out, small[5], small[6], small[7],
        up, small[8:12].reshape(-1), down, small[12],
    )


def solution(mesh):
    rows = P(("dp", "tensor"), None)
    return jax.shard_map(
        on_device,
        mesh=mesh,
        in_specs=(
            rows, P("dp", None), P(), P(), P(None, None, "tensor"), P(None, "tensor"), P("tensor", None), P(),
            P(), P(), P(None, "tensor"), P("tensor"), P("tensor", None), P(), rows,
        ),
        out_specs=(
            rows, rows, P(), P(), P(None, "dp", "tensor"), P(), P("tensor", "dp"), P(), P(), P(),
            P("dp", "tensor"), P(), P("tensor", "dp"), P(),
        ),
        check_vma=False,
    )
```

time: 1120 us -> 235 us (0.21)
  waiting for transfers between devices: 670 us -> 0 us
  Pallas kernels: 0 us -> 221 us
  matrix products: 186 us -> 0 us
  other arithmetic: 97.8 us -> 0.77 us
  local copies, waits for them, and re-layouts: 90.2 us -> 12.2 us
  blocking collectives: 45.4 us -> 0 us
  between operations: 15.9 us -> 0.67 us
    reduce_scatter x7 -> x0, waiting for transfers between devices: 459 us -> none  [the longest x1 183 us: on_device(): lax.psum_scatter(grad_up_weight, 'dp', scatter_dimension=0, tiled=True)]
    pallas_call x0 -> x1, Pallas kernels: none -> 221 us  [on_device(): pl.pallas_call(functools.partial(kernel, dp), out_shape=(jax.ShapeDtypeSt...]
    dot_general x26 -> x0, matrix products: 186 us -> none  [the longest x1 28.4 us: on_device(): jnp.einsum('pd,fd->pf', cot_full, down_weight, preferred_element_type=jnp...]
    unnamed x13 -> x0, waiting for transfers between devices: 173 us -> none
    psum x1 -> x0, blocking collectives: 45.4 us -> none  [on_device(): lax.psum((grad_attn_gain, grad_attn_shift, full_proj_bias, grad_out_bias,...]
    convert_element_type x9 -> x0, other arithmetic: 44.1 us -> none  [the longest x2 25 us: backward_block(): grad_scores = (attention * (grad_attention - inner)).astype(jnp.bfloat16)]
    concatenate x2 -> x0, local copies, waits for them, and re-layouts: 40 us -> none  [rotate(): return jnp.concatenate(pieces, axis=-1)]
    all_gather x4 -> x0, waiting for transfers between devices: 37.4 us -> none  [the longest x1 12.1 us: on_device(): lax.all_gather(normed_one.astype(jnp.bfloat16), 'tensor', axis=0, tiled=T...]
  transfers between devices with their start and end apart: 12 -> 0, of which waited for: 10 -> 0; matrix products, arithmetic and copies ran while one was open for 8% -> 0% of each run, Pallas kernels for 0% -> 0%
where the time goes in v1:
time: 235 us
  Pallas kernels  221 us (94%)
  local copies, waits for them, and re-layouts  12.2 us (5%)
    pallas_call x1, Pallas kernels, on_device(): pl.pallas_call(functools.partial(kernel, dp), out_shape=(jax.ShapeDtypeSt...  221 us
    unnamed x9, local copies, waits for them, and re-layouts  4.96 us

profile of v1, /device:TPU:0, one launch (start us, length us, event | category | flops | bytes accessed | tf_op | source)
XLA Modules:
  0.0 234.7 jit_solution(4258413451576727446)
XLA Ops:
  0.6 1.3 copy.30
  1.9 221.1 %block.1 = (bf16[512,1024]{1,0:T(8,128)(2,1)}, f32[512,1024]{1,0:T(8,128)}, f32[64,6144]{1,0:T(8,128)}, f32[16,1024]{1,0:T(8,128)}) custom-call(bf16[512,1024]{1,0:T(8,128)(2,1)} %tok_h.1, bf16[512,1024]{1,0:T(8,128)(2,1)} %cot_h.1, bf16[3,1024,512]{2,1,0:T(8,128)(2,1)} %pw_h.1, bf16[512,1024]{1,0:T(8,128)(2,1)} %ow_h.1, bf16[1024,2048]{1,0:T(8,128)(2,1)} %uw_h.1, ...), custom_call_target="tpu_custom_call" | custom-call | tf_op jit(solution)/shard_map/block/pallas_call | solution.py:746
  223.0 0.0 copy-start.1
  223.0 1.5 slice.47
  224.5 0.8 slice_bitcast_fusion.5
  225.2 1.6 fusion
  226.8 0.6 copy.33
  227.4 1.8 slice_bitcast_fusion.1
  229.2 0.0 copy-start
  229.2 2.4 %slice_bitcast_fusion = (f32[2048,64]{0,1:T(8,128)}, f32[64,2048]{1,0:T(8,128)}) fusion(f32[64,6144]{1,0:T(8,128)} %get-tuple-element.21), kind=kLoop, calls=%fused_computation | loop fusion | bytes 2097152 | tf_op jit(solution)/shard_map/transpose | solution.py:766
  231.6 0.8 pad_maximum_fusion
  232.4 0.0 copy-done.1
  232.4 1.0 copy.36
  233.4 0.0 copy-done
  233.4 1.3 copy.37
Async XLA Ops:
  223.0 9.4 %copy-start.1 = (bf16[512,1024]{1,0:T(8,128)(2,1)S(1)}, bf16[512,1024]{1,0:T(8,128)(2,1)}, u32[]{:S(2)}) copy-start(bf16[512,1024]{1,0:T(8,128)(2,1)} %get-tuple-element.48) | copy-start | bytes 3145732
  229.2 4.2 %copy-start = (f32[512,1024]{1,0:T(8,128)S(1)}, f32[512,1024]{1,0:T(8,128)}, u32[]{:S(2)}) copy-start(f32[512,1024]{1,0:T(8,128)} %get-tuple-element.49) | copy-start | bytes 6291460

commit v2 on v1

v2 whole, which is shorter than its diff:
```python
import functools
import math

import jax
import jax.numpy as jnp
import ml_dtypes
import numpy as np
from jax import lax
from jax.experimental import pallas as pl
from jax.experimental.pallas import tpu as pltpu
from jax.sharding import PartitionSpec as P

HEAD = 64
GRID = 16
FRAME = 258
EPS = 1e-6
LANES = 128
FC = 256
MESH = pl.DeviceIdType.MESH
F32 = jnp.float32
BF = jnp.bfloat16
NEG = -1e30
FRAMES = 4
TERM = 16


def nn(a, b):
    return jnp.dot(a, b, preferred_element_type=F32)


def nt(a, b):
    return lax.dot_general(a, b, (((1,), (1,)), ((), ())), preferred_element_type=F32)


def rope_tables():
    side = 2 * (HEAD // 6)
    sections = (HEAD - 2 * side, side, side)
    cos = np.zeros((FRAMES + 2 * GRID, HEAD), np.float64)
    sin = np.zeros((FRAMES + 2 * GRID, HEAD), np.float64)
    lane, row = 0, 0
    for width, count in zip(sections, (FRAMES, GRID, GRID)):
        half = width // 2
        freq = np.float32(10000.0) ** (-np.arange(half, dtype=np.float32) * np.float32(2.0) / np.float32(width))
        angle = (np.arange(count, dtype=np.float32)[:, None] * freq.astype(np.float32)[None, :]).astype(np.float64)
        cos[row : row + count, lane : lane + half] = np.cos(angle)
        cos[row : row + count, lane + half : lane + width] = np.cos(angle)
        sin[row : row + count, lane : lane + half] = -np.sin(angle)
        sin[row : row + count, lane + half : lane + width] = np.sin(angle)
        lane, row = lane + width, row + count
    both = np.concatenate([cos, cos, sin, sin], axis=1).astype(np.float32)
    out = np.zeros((LANES, 4 * HEAD), ml_dtypes.bfloat16)
    rest, n = both, both.shape[0]
    for term in range(3):
        part = rest.astype(ml_dtypes.bfloat16)
        out[term * n : (term + 1) * n] = part
        rest = rest - part.astype(np.float32)
    return out


def partner_of(x, lane):
    side = 2 * (HEAD // 6)
    first = HEAD - 2 * side
    a, b = first // 2, side // 2
    within = lane % HEAD
    past = (within - first) % side
    up_a = pltpu.roll(x, LANES - a, 1)
    down_a = pltpu.roll(x, a, 1)
    up_b = pltpu.roll(x, LANES - b, 1)
    down_b = pltpu.roll(x, b, 1)
    in_first = jnp.where(within < a, up_a, down_a)
    in_side = jnp.where(past < b, up_b, down_b)
    return jnp.where(within < first, in_first, in_side)


def split3(x):
    hi = x.astype(BF).astype(F32)
    mid = (x - hi).astype(BF).astype(F32)
    return hi, mid, x - hi - mid


def kernel(
    dp, tok_h, cot_h, pw_h, ow_h, uw_h, dw_h, lens, gain1, shift1, pbias, obias, gain2, shift2, ubias, dbias, table,
    mixed_h, gtok_h, g_down, g_up, g_out, g_proj, small, U, DN, OW, TOKX, N1, T1, T2, CG, N2, QA, K, V, ATT, ACT, GH, MID, X1, S1,
    ONE, QF, KF, SB, SBR, WIDE, G, *rest,
):
    stages = dp.bit_length() - 1
    RM, RP = rest[:stages], rest[stages : 2 * stages]
    m_send, m_recv, p_send, p_recv, x_send, x_recv, b_send, b_recv, loads = rest[2 * stages :]
    T = tok_h.shape[0]
    D = tok_h.shape[1]
    R = 2 * T
    E = OW.shape[0]
    F = DN.shape[0]
    pairs = E // LANES
    nf = F // FC
    low = stages - 4
    unit = 1 << low
    me = lax.axis_index("dp")
    core = lax.axis_index("tensor")
    lane = lax.broadcasted_iota(jnp.int32, (1, LANES), 1)

    def bit_of(stride):
        return (me // stride) % 2

    def partner(stride):
        return me + (1 - 2 * bit_of(stride)) * stride

    def load(src, dst, k):
        return pltpu.make_async_copy(src, dst, loads.at[k])

    tok_load = load(tok_h, TOKX, 0)
    cot_load = load(cot_h, CG.at[pl.ds(0, T)], 1)
    ow_load = load(ow_h, OW, 2)
    uw_load = load(uw_h, U, 3)
    dw_load = load(dw_h, DN, 4)
    tok_again = load(tok_h, N2.at[pl.ds(0, T)], 5)
    mixed_store = load(N2.at[pl.ds(0, T)], mixed_h, 6)

    def projection_loads(k):
        return [
            load(
                pw_h.at[c, :, pl.ds(p * LANES, LANES)], U.at[:, pl.ds((3 * p + c) * LANES, LANES)],
                k + 3 * p + c,
            )
            for p in range(pairs)
            for c in range(3)
        ]

    pw_loads = projection_loads(8)
    pw_again = projection_loads(8 + 3 * pairs)

    def gtok_store(m):
        rows = pl.ds(m * (T // 2), T // 2)
        return load(WIDE.at[m], gtok_h.at[rows], 8 + 6 * pairs + m)

    tok_load.start()
    for c in pw_loads:
        c.start()
    cot_load.start()
    ow_load.start()
    dw_load.start()

    barrier = pltpu.get_barrier_semaphore()
    peers = [(partner(1 << b), core) for b in range(stages)] + [(me, 1 - core)]
    for who in peers:
        pl.semaphore_signal(barrier, inc=1, device_id=who, device_id_type=MESH)

    @pl.loop(0, R // 256)
    def _(m):
        row = lax.broadcasted_iota(jnp.int32, (256, 1), 0) + m * 256
        place = row + core * T
        place = jnp.where(place >= R, place - R, place)
        begin = jnp.zeros((256, 1), jnp.int32)
        episode = jnp.zeros((256, 1), jnp.int32)
        end = jnp.int32(0)
        for e in range(lens.shape[1] - 1):
            end = end + lens[0, e]
            begin = jnp.where(place >= end, end, begin)
            episode = jnp.where(place >= end, e + 1, episode)
        local = place - begin
        frame = jnp.zeros((256, 1), jnp.int32)
        for k in range(1, FRAMES):
            frame = jnp.where(local >= k * FRAME, k, frame)
        inside = local - frame * FRAME
        patch = jnp.maximum(inside - 2, 0)
        row_pos = jnp.where(inside >= 2, patch // GRID, 0)
        col_pos = jnp.where(inside >= 2, patch % GRID, 0)
        n = FRAMES + 2 * GRID
        spot = lane % n
        hit = (spot == frame) | (spot == FRAMES + row_pos) | (spot == FRAMES + GRID + col_pos)
        hit = hit & (lane < 3 * n)
        rows = pl.ds(m * 256, 256)
        ONE[rows] = jnp.where(hit, 1.0, 0.0).astype(BF)
        feature = lane % HEAD
        counted = (feature // FRAMES == episode) & (feature % FRAMES <= frame)
        is_class = feature < TERM
        QF[rows] = jnp.where(is_class & jnp.logical_not(counted), NEG, 0.0).astype(BF)
        ones = (feature == episode * FRAMES + frame) | ((feature >= TERM) & (feature < TERM + 3))
        KF[rows] = jnp.where(ones, 1.0, 0.0).astype(BF)

    def cross(src, dst, k):
        return pltpu.make_async_remote_copy(
            src_ref=src, dst_ref=dst, send_sem=x_send.at[k], recv_sem=x_recv.at[k],
            device_id=(me, 1 - core), device_id_type=MESH,
        )

    half = T // 2

    def turned(dst, src, first, count):
        @pl.loop(first // 256, (first + count) // 256)
        def _(m):
            rows = pl.ds(pl.multiple_of(m * 256, 256), 256)
            dst[:, rows] = src[rows].T

    def cross_rows(src, s0, dst, d0, base, m):
        return cross(src.at[pl.ds(s0 + m * half, half)], dst.at[pl.ds(d0 + m * half, half)], base + m)

    def order_of(kind, par):
        where = {"x": unit * (1 + par), "y": unit * (2 - par), "z": unit * 4, "Z": unit * 8}
        return [where[k] for k in kind + "Z"] + [1 << b for b in reversed(range(low))]

    def places_of(kind, par):
        w = {k: 8 >> i for i, k in enumerate(kind + "Z")}
        return (w["x"] + par * (w["y"] - w["x"]), w["y"] + par * (w["x"] - w["y"]), w["z"], w["Z"])

    def g_view(fam, c):
        if fam == "M":
            return G.at[(2 * c[0] + c[1]) % 8]
        if fam == "O":
            return G.at[2 + c]
        p, k = c
        return G.at[p + 4 * (k // 2), :, pl.ds((k % 2) * LANES, LANES)]

    def slot(fam, c):
        if fam == "M":
            return RM, 2 * c[0] + c[1], m_send, m_recv
        if fam == "O":
            return RM, 2 * nf + c, m_send, m_recv
        return RP, 3 * c[0] + c[1], p_send, p_recv

    block = D // 16

    def put(fam, c, value, row0, kind, par):
        w = places_of(kind, par)
        view = g_view(fam, c)
        for b in range(value.shape[0] // block):
            n = row0 * (value.shape[0] // block) + b
            place = ((n % 2) * w[0] + ((n // 2) % 2) * w[1] + ((n // 4) % 2) * w[2] + (n // 8) * w[3]) * block
            view[pl.ds(pl.multiple_of(place, block), block), :] = value[b * block : (b + 1) * block].astype(BF)

    def rs_parts(fam, c, s, order):
        R_, at, ss, rr = slot(fam, c)
        view = g_view(fam, c) if s == 0 else R_[s - 1].at[at]
        n = D >> s
        h = n // 2
        bit = bit_of(order[s])
        if h >= 16:
            src = view.at[pl.ds(pl.multiple_of((1 - bit) * h, 16), h)]
            keep = view.at[pl.ds(pl.multiple_of(bit * h, 16), h)]
        else:
            src = keep = view
        copy = pltpu.make_async_remote_copy(
            src_ref=src, dst_ref=R_[s].at[at], send_sem=ss.at[at, s], recv_sem=rr.at[at, s],
            device_id=(partner(order[s]), core), device_id_type=MESH,
        )
        return copy, keep, R_[s].at[at], bit, h

    def finish(fam, c, total):
        if fam == "M":
            into = g_down if c[1] == 0 else g_up
            into[:, pl.ds(pl.multiple_of(c[0] * FC, FC), FC)] = total
        elif fam == "O":
            g_out[:, c * FC : (c + 1) * FC] = total
        else:
            g_proj[c[1], :, pl.ds(pl.multiple_of(c[0] * LANES, LANES), LANES)] = total

    def rs_start(fam, c, s, order):
        rs_parts(fam, c, s, order)[0].start()

    def rs_step(fam, c, s, order):
        copy, keep, landed, bit, h = rs_parts(fam, c, s, order)
        copy.wait()
        if s < stages - 1:
            n = landed.shape[0]
            piece = min(n, 64)
            if n == piece:
                landed[...] = landed[...] + keep[...]
            else:
                @pl.loop(0, n // piece)
                def _(q):
                    at = pl.ds(pl.multiple_of(q * piece, piece), piece)
                    landed[at] = landed[at] + keep[at]

            rs_start(fam, c, s + 1, order)
        else:
            total = landed[...].astype(F32) + keep[...].astype(F32)
            if h < 16:
                total = jnp.where(bit == 1, total[8:], total[:8])
            finish(fam, c, total)

    plan = make_plan(stages, nf, pairs)

    def poll(point, at=None):
        if at is None:
            for fam, c, s in plan.pop((point, 0), ()):
                rs_step(fam, c, s, order_of(*kind_of(fam, c)))
            return
        for k in sorted(k for p, k in plan if p == point):
            @pl.when(at == k)
            def _():
                for fam, c, s in plan.pop((point, k)):
                    rs_step(fam, c, s, order_of(*kind_of(fam, c)))

    def normed(x):
        centre = x - jnp.mean(x, axis=1, keepdims=True)
        inv = lax.rsqrt(jnp.mean(centre * centre, axis=1, keepdims=True) + EPS)
        return centre * inv, inv

    tok_load.wait()

    @pl.loop(0, 2)
    def _(m):
        @pl.loop(0, half // 128)
        def _(q):
            rows = pl.ds(m * half + q * 128, 128)
            x = TOKX[rows].astype(F32)
            N1[rows] = (normed(x)[0] * gain1[...] + shift1[...]).astype(BF)

    def rotary(rows):
        both = nn(ONE[rows], table[...])
        return both[:, :LANES], both[:, LANES:]

    for c in pw_loads:
        c.wait()

    def project(m):
        rows = pl.ds(m * 256, 256)
        x = N1[rows]
        cos, sin = rotary(rows)
        all_three = nn(x, U[:, : 3 * E])
        for p in range(pairs):
            q, k, v = (
                all_three[:, (3 * p + c) * LANES : (3 * p + c + 1) * LANES]
                + pbias[c : c + 1, p * LANES : (p + 1) * LANES]
                for c in range(3)
            )
            q = ((q * cos + partner_of(q, lane) * sin) * HEAD**-0.5).astype(BF)
            QA[2 * p, rows] = jnp.where(lane < HEAD, q, QF[rows])
            QA[2 * p + 1, rows] = jnp.where(lane >= HEAD, q, QF[rows])
            K[rows, p * LANES : (p + 1) * LANES] = (k * cos + partner_of(k, lane) * sin).astype(BF)
            V[rows, p * LANES : (p + 1) * LANES] = v.astype(BF)

    @pl.loop(0, 2)
    def _(m):
        project(m)

    cot_load.wait()
    pl.semaphore_wait(barrier, len(peers))

    @pl.loop(0, 2)
    def _(m):
        cross_rows(N1, 0, N1, T, 1, m).start()

    cot_send = cross(CG.at[pl.ds(0, T)], CG.at[pl.ds(T, T)], 0)
    cot_send.start()
    turned(T1, CG, 0, T)

    @pl.loop(0, 2)
    def _(m):
        cross_rows(N1, 0, N1, T, 1, m).wait()
        project(2 + m)

    uw_load.start()

    def mine(e):
        return lane < HEAD if e == 0 else lane >= HEAD

    def key_sets(p, box):
        cols = pl.ds(pl.multiple_of(p * LANES, LANES), LANES)
        for e in range(2):
            box[:, e * LANES : (e + 1) * LANES] = jnp.where(mine(e), K[:, cols], KF[...])
            box[:, (2 + e) * LANES : (3 + e) * LANES] = jnp.where(mine(e), V[:, cols], jnp.ones((), BF))

    def attend(first):
        @pl.loop(0, pairs)
        def _(p):
            key_sets(p, T2)

            @pl.loop(0, T // 256, unroll=2)
            def _(b):
                rows = pl.ds(first + b * 256, 256)
                parts = []
                for e in range(2):
                    qa = QA[2 * p + e, rows]
                    s = nt(qa, T2[:, e * LANES : (e + 1) * LANES])
                    top = jnp.max(s, axis=1, keepdims=True)
                    w = jnp.exp(s - top).astype(BF)
                    o = nn(w, T2[:, (2 + e) * LANES : (3 + e) * LANES])
                    parts.append(o / pltpu.roll(o, HEAD, 1))
                    total = jnp.where(mine(e), 1.0, o)
                    hi, mid, lo = split3(top + jnp.log(total))
                    feature = lane % HEAD
                    terms = jnp.where(feature == TERM, -hi, jnp.where(feature == TERM + 1, -mid, -lo)).astype(BF)
                    is_term = (feature >= TERM) & (feature < TERM + 3) & jnp.logical_not(mine(e))
                    QA[2 * p + e, rows] = jnp.where(is_term, terms, qa)
                ATT[rows, pl.ds(pl.multiple_of(p * LANES, LANES), LANES)] = jnp.where(
                    lane < HEAD, parts[0], parts[1]
                ).astype(BF)

    attend(T)
    ow_load.wait()

    @pl.loop(0, 2)
    def _(m):
        rows = pl.ds(m * half, half)
        S1[rows] = nn(ATT[pl.ds(T + m * half, half)], OW[...]).astype(BF)
        cross_rows(S1, 0, X1, 0, 3, m).start()

    attend(0)

    @pl.loop(0, 2)
    def _(m):
        rows = pl.ds(m * half, half)
        MID[rows] = nn(ATT[rows], OW[...])
        cross_rows(S1, 0, X1, 0, 3, m).wait()

        @pl.loop(0, half // 128)
        def _(q):
            rows = pl.ds(m * half + q * 128, 128)
            mid = TOKX[rows].astype(F32) + (MID[rows] + X1[rows].astype(F32) + obias[...])
            MID[rows] = mid
            N2[rows] = (normed(mid)[0] * gain2[...] + shift2[...]).astype(BF)

        cross_rows(N2, 0, N2, T, 5, m).start()

    SB[...] = jnp.zeros_like(SB)
    SB[15:16] = jnp.sum(CG[0:T].astype(F32), axis=0, keepdims=True)
    turned(T2, N2, 0, T)
    cot_send.wait()
    turned(T1, CG, T, T)

    @pl.loop(0, 2)
    def _(m):
        cross_rows(N2, 0, N2, T, 5, m).wait()

    turned(T2, N2, T, T)
    uw_load.wait()
    dw_load.wait()

    ones8 = jnp.ones((8, R), BF)

    wide = 2 * FC

    @pl.loop(0, nf // 2)
    def _(j):
        cols = pl.ds(pl.multiple_of(j * wide, wide), wide)

        @pl.loop(0, R // 256)
        def _(m):
            rows = pl.ds(m * 256, 256)
            h = nn(N2[rows], U[:, cols]) + ubias[:, cols]
            cdf = 0.5 + 0.5 * lax.erf(h * math.sqrt(0.5))
            ACT[rows, cols] = (h * cdf).astype(BF)
            slope = cdf + h * jnp.exp(h * h * -0.5) * (1.0 / math.sqrt(2 * math.pi))
            GH[rows, cols] = (nt(CG[rows], DN[cols]) * slope).astype(BF)

        poll("hidden", j)
        for k, (left, right) in enumerate(((T1, ACT), (T2, GH))):
            @pl.loop(0, D // 512)
            def _(m):
                both = nn(left[pl.ds(m * 512, 512)], right[:, cols])
                for e in range(2):
                    put("M", (2 * j + e, k), both[:, e * FC : (e + 1) * FC], m, M_KINDS[2 * e + k], j % 2)

            for e in range(2):
                rs_start("M", (2 * j + e, k), 0, order_of(M_KINDS[2 * e + k], j % 2))
            poll("down" if k == 0 else "up", j)

        sums = nn(ones8, GH[:, cols])
        per = D // wide
        SB[pl.ds(11 + core * (F // D) + j // per, 1), pl.ds(pl.multiple_of((j % per) * wide, wide), wide)] = sums[0:1]
    tok_again.start()

    def norm_back(g, x, gain, row):
        xhat, inv = normed(x)
        SB[row : row + 1] += jnp.sum(g * xhat, axis=0, keepdims=True)
        SB[row + 1 : row + 2] += jnp.sum(g, axis=0, keepdims=True)
        gx = g * gain
        a = jnp.mean(gx, axis=1, keepdims=True)
        b = jnp.mean(gx * xhat, axis=1, keepdims=True)
        return inv * (gx - a - xhat * b)

    @pl.loop(0, 2)
    def _(m):
        S1[pl.ds(m * half, half)] = nt(GH[pl.ds(T + m * half, half)], U[...]).astype(BF)
        cross_rows(S1, 0, X1, 0, 7, m).start()

    poll("norm")

    @pl.loop(0, 2)
    def _(m):
        WIDE[0] = nt(GH[pl.ds(m * half, half)], U[...])
        cross_rows(S1, 0, X1, 0, 7, m).wait()

        @pl.loop(0, half // 64)
        def _(q):
            at = pl.ds(m * half + q * 64, 64)
            g = WIDE[0, pl.ds(q * 64, 64)] + X1[at].astype(F32)
            total = CG[at].astype(F32) + norm_back(g, MID[at], gain2[...], 9)
            high = total.astype(BF)
            CG[at] = high
            TOKX[at] = (total - high.astype(F32)).astype(BF)
            SB[8:9] += jnp.sum(high.astype(F32), axis=0, keepdims=True)

        cross_rows(CG, 0, CG, T, 9, m).start()
        poll("branch", m)

    for c in pw_again:
        c.start()

    def grad_attended(m):
        rows = pl.ds(m * half, half)
        GH[rows, 0:E] = nt(CG[rows], OW[...]).astype(BF)

    @pl.loop(0, 2)
    def _(m):
        grad_attended(m)

    turned(T1, CG, 0, T)
    poll("attended")

    @pl.loop(0, 2)
    def _(m):
        cross_rows(CG, 0, CG, T, 9, m).wait()
        grad_attended(2 + m)

    turned(T1, CG, T, T)

    @pl.loop(0, D // 512)
    def _(m):
        both = nn(T1[pl.ds(m * 512, 512)], ATT[...])
        for c in range(2):
            put("O", c, both[:, c * FC : (c + 1) * FC], m, O_KINDS[c], 0)

    for c in range(2):
        rs_start("O", c, 0, order_of(O_KINDS[c], 0))
    turned(T2, N1, 0, R)
    poll("out")

    def sums(g, s):
        who = (partner(1 << s), core) if s < stages else (me, 1 - core)
        return pltpu.make_async_remote_copy(
            src_ref=SB.at[pl.ds(8 * g, 8)], dst_ref=SBR.at[g, s],
            send_sem=b_send.at[g, s], recv_sem=b_recv.at[g, s],
            device_id=who, device_id_type=MESH,
        )

    def sum_start(g, s):
        sums(g, s).start()

    def sum_step(g, s):
        sums(g, s).wait()
        SB[8 * g : 8 * g + 8] = SB[8 * g : 8 * g + 8] + SBR[g, s]
        if s < stages:
            sum_start(g, s + 1)

    def key_grads(b, k):
        return pl.ds(pl.multiple_of((2 * b + k) * LANES, LANES), LANES)

    sum_start(1, 0)
    @pl.loop(0, pairs)
    def _(p):
        cols = pl.ds(pl.multiple_of(p * LANES, LANES), LANES)
        key_sets(p, T1)
        N1[0:LANES] = K[:, cols].T
        for e in range(2):
            @pl.loop(0, R // 256)
            def _(b):
                rows = pl.ds(b * 256, 256)
                g = GH[rows, cols]
                both = g.astype(F32) * ATT[rows, cols].astype(F32)
                inner = jnp.sum(jnp.where(mine(e), both, 0.0), axis=1, keepdims=True)
                hi, mid, lo = split3(inner)
                feature = lane % HEAD
                terms = jnp.where(feature == TERM, -hi, jnp.where(feature == TERM + 1, -mid, -lo))
                is_term = (feature >= TERM) & (feature < TERM + 3)
                terms = jnp.where(is_term, terms, 0.0).astype(BF)
                T1[rows, (4 + e) * LANES : (5 + e) * LANES] = jnp.where(mine(e), g, terms)

        for e in range(2):
            WIDE[1, e * HEAD : (e + 1) * HEAD] = jnp.zeros((HEAD, R), F32)

        poll("keys", p)

        @pl.loop(0, R // 256)
        def _(b):
            rows = pl.ds(b * 256, 256)
            pair = []
            for e in range(2):
                dk = dv = 0.0
                for a in range(2):
                    across = pl.ds(a * T, T)
                    qa = QA[2 * p + e, across]
                    ga = T1[across, (4 + e) * LANES : (5 + e) * LANES]
                    w = jnp.exp(nt(T1[rows, e * LANES : (e + 1) * LANES], qa))
                    ds = (w * nt(T1[rows, (2 + e) * LANES : (3 + e) * LANES], ga)).astype(BF)
                    dv += nn(w.astype(BF), ga)
                    dk += nn(ds, qa)
                    WIDE[1, e * HEAD : (e + 1) * HEAD, across] += nn(N1[e * HEAD : (e + 1) * HEAD, rows], ds)
                pair.append((dk, dv))
            for k, (g0, g1) in enumerate(zip(*pair)):
                WIDE[0, :, key_grads(b, k)] = jnp.where(mine(0), g0, g1)
            poll("inner", p * (R // 256) + b)

        @pl.loop(0, R // 256)
        def _(b):
            rows = pl.ds(b * 256, 256)
            cos, sin = rotary(rows)

            def back(g):
                g = g.astype(BF).astype(F32)
                return g * cos - partner_of(g, lane) * sin

            parts = (
                back(WIDE[1, 0:LANES, rows].T) * HEAD**-0.5,
                back(WIDE[0, :, key_grads(b, 0)]),
                WIDE[0, :, key_grads(b, 1)],
            )
            for c, part in enumerate(parts):
                GH[rows, pl.ds(pl.multiple_of(E + (3 * p + c) * LANES, LANES), LANES)] = part.astype(BF)

        own_cols = pl.ds(pl.multiple_of(E + 3 * p * LANES, LANES), 3 * LANES)

        @pl.loop(0, D // 512)
        def _(m):
            three = nn(T2[pl.ds(m * 512, 512)], GH[:, own_cols])
            for c in range(3):
                put("P", (p, c), three[:, c * LANES : (c + 1) * LANES], m, P_KINDS[c], 0)

        for c in range(3):
            rs_start("P", (p, c), 0, order_of(P_KINDS[c], 0))
        totals = nn(ones8, GH[:, own_cols])[0:1]
        for c in range(3):
            at = pl.multiple_of(core * E + p * LANES, LANES)
            SB[2 + c : 3 + c, pl.ds(at, LANES)] = totals[:, c * LANES : (c + 1) * LANES]

        poll("pair", p)
        for q in range(min(pairs, stages + 1)):
            @pl.when(p == q)
            def _():
                sum_step(1, q)

    for c in pw_again:
        c.wait()

    @pl.loop(0, 2)
    def _(m):
        S1[pl.ds(m * half, half)] = nt(GH[pl.ds(T + m * half, half), E : 4 * E], U[:, : 3 * E]).astype(BF)
        cross_rows(S1, 0, X1, 0, 13, m).start()

    poll("input")
    tok_again.wait()

    @pl.loop(0, 2)
    def _(m):
        rows = pl.ds(m * half, half)
        WIDE[m] = nt(GH[rows, E : 4 * E], U[:, : 3 * E])
        cross_rows(S1, 0, X1, 0, 13, m).wait()

        @pl.loop(0, half // 64)
        def _(q):
            at = pl.ds(m * half + q * 64, 64)
            here = pl.ds(q * 64, 64)
            g = WIDE[m, here] + X1[at].astype(F32)
            before = CG[at].astype(F32) + TOKX[at].astype(F32)
            WIDE[m, here] = before + norm_back(g, N2[at].astype(F32), gain1[...], 0)


        gtok_store(m).start()

    sum_start(0, 0)

    poll("tokens")

    @pl.loop(0, 2)
    def _(m):
        S1[pl.ds(m * half, half)] = nn(ACT[pl.ds(T + m * half, half)], DN[...]).astype(BF)
        cross_rows(S1, 0, N2, T, 11, m).start()

    early = list(range(pairs, stages + 1))
    if early:
        sum_step(1, early.pop(0))
    sum_step(0, 0)
    poll("mixed")

    @pl.loop(0, 2)
    def _(m):
        rows = pl.ds(m * half, half)
        MID[rows] += nn(ACT[rows], DN[...])
        cross_rows(S1, 0, N2, T, 11, m).wait()

        @pl.loop(0, half // 64)
        def _(q):
            at = pl.ds(m * half + q * 64, 64)
            other = N2[pl.ds(T + m * half + q * 64, 64)].astype(F32)
            N2[at] = (MID[at] + (other + dbias[...])).astype(BF)

    mixed_store.start()
    for s in range(1, stages + 1):
        if early:
            sum_step(1, early.pop(0))
        sum_step(0, s)
        poll("last%d" % s)
    poll("rest")
    assert not plan
    small[...] = SB[...]
    mixed_store.wait()
    for m in range(2):
        gtok_store(m).wait()


def hand_over(*refs):
    arrive = [pltpu.make_async_copy(refs[k], refs[-8 + k], refs[-2].at[k]) for k in range(6)]
    leave = [pltpu.make_async_copy(refs[-8 + k], refs[7 + k], refs[-1].at[k]) for k in range(6)]
    for c in arrive:
        c.start()
    small, vectors = refs[6], refs[13:21]
    for v, at in zip(vectors, (0, 1, 8, 9, 10, 15)):
        v[...] = small[at : at + 1]
    vectors[6][...] = small[2:5]
    vectors[7][...] = small[11:15]
    for k in range(6):
        arrive[k].wait()
        leave[k].start()
    for c in leave:
        c.wait()


M_KINDS = ("xyz", "yzx", "zxy", "yxz")
O_KINDS = ("xzy", "zyx")
P_KINDS = ("xyz", "yzx", "zxy")


def kind_of(fam, c):
    if fam == "M":
        return M_KINDS[2 * (c[0] % 2) + c[1]], (c[0] // 2) % 2
    if fam == "O":
        return O_KINDS[c], 0
    return P_KINDS[c[1]], 0


def make_plan(stages, nf, pairs):
    now, free, flying, plan = 0.0, {}, {}, {}

    def send(fam, c, s):
        kind, par = kind_of(fam, c)
        axes = [a if not par or a == "z" else "yx"["xy".index(a)] for a in kind] + ["z"] + ["w"] * stages
        size = (FC if fam != "P" else LANES) / FC * WIRE / 2**s
        begin = max(now, free.get(axes[s], 0.0))
        free[axes[s]] = begin + size
        flying[(fam, c, s)] = begin + size + LATENCY

    def take(point, at, only=None, everything=False):
        nonlocal now
        while True:
            ready = [
                (t, k) for k, t in flying.items()
                if (everything or t <= now + SLACK or (only and only(k))) and (only is None or only(k))
            ]
            if not ready:
                return
            t, k = min(ready)
            del flying[k]
            now = max(now, t) + STEP
            plan.setdefault((point, at), []).append(k)
            if k[2] < stages - 1:
                send(k[0], k[1], k[2] + 1)

    def first(k):
        return k[0] == "M" and k[2] == 0

    for j in range(nf // 2):
        now += TIMES["hidden"]
        take("hidden", j, lambda k: first(k) and k[1][0] // 2 <= j - 2)
        take("hidden", j)
        for k, point in enumerate(("down", "up")):
            now += TIMES[point]
            for e in range(2):
                send("M", (2 * j + e, k), 0)
            take(point, j)
    now += TIMES["norm"]
    take("norm", 0)
    for m in range(2):
        now += TIMES["branch"]
        take("branch", m)
    now += TIMES["attended"]
    take("attended", 0, lambda k: first(k) and k[1][0] == nf - 3)
    take("attended", 0)
    now += TIMES["out"]
    for c in range(2):
        send("O", c, 0)
    take("out", 0)
    for p in range(pairs):
        now += TIMES["keys"]
        if p == 0:
            take("keys", p, first)
        if p == 2:
            take("keys", p, lambda k: k[0] == "O" and k[2] == 0)
        take("keys", p)
        for b in range(4):
            now += TIMES["inner"]
            take("inner", 4 * p + b)
        now += TIMES["pair"]
        for c in range(3):
            send("P", (p, c), 0)
        take("pair", p)
    for point in ("input", "tokens", "mixed"):
        now += TIMES[point]
        take(point, 0)
    now += TIMES["last"]
    for s in range(1, stages + 1):
        now += 2.0
        take("last%d" % s, 0)
    take("rest", 0, everything=True)
    return plan


WIRE = 8.0
LATENCY = 6.0
SLACK = 0.0
STEP = 0.3
TIMES = dict(
    hidden=3.0, down=1.5, up=1.6, norm=2.6, branch=2.5, attended=1.8, out=4.0, keys=2.4, inner=1.7,
    pair=3.0, input=1.8, tokens=4.0, mixed=2.6, last=3.0,
)


def on_device(
    tokens, episode_lengths, attn_gain, attn_shift, proj_weight, proj_bias, out_weight, out_bias,
    mlp_gain, mlp_shift, up_weight, up_bias, down_weight, down_bias, cotangent,
):
    dp = lax.axis_size("dp")
    stages = dp.bit_length() - 1
    T, D = tokens.shape
    R = 2 * T
    E = proj_weight.shape[2]
    F = up_weight.shape[1]
    pairs = E // LANES
    nf = F // FC
    row = lambda v: v.reshape(1, -1).astype(F32)
    rows_at = [max(D >> (s + 1), 16) for s in range(stages)]
    vmem = pl.BlockSpec(memory_space=pltpu.VMEM)
    hbm = pl.BlockSpec(memory_space=pl.ANY)
    smem = pl.BlockSpec(memory_space=pltpu.SMEM)
    dma = pltpu.SemaphoreType.DMA
    scratch = [
        pltpu.VMEM((D, F), BF),
        pltpu.VMEM((F, D), BF),
        pltpu.VMEM((E, D), BF),
        pltpu.VMEM((T, D), BF),
        pltpu.VMEM((R, D), BF),
        pltpu.VMEM((D, R), BF),
        pltpu.VMEM((D, R), BF),
        pltpu.VMEM((R, D), BF),
        pltpu.VMEM((R, D), BF),
        pltpu.VMEM((2 * pairs, R, LANES), BF),
        pltpu.VMEM((R, E), BF),
        pltpu.VMEM((R, E), BF),
        pltpu.VMEM((R, E), BF),
        pltpu.VMEM((R, F), BF),
        pltpu.VMEM((R, F), BF),
        pltpu.VMEM((T, D), F32),
        pltpu.VMEM((T, D), BF),
        pltpu.VMEM((T, D), BF),
        pltpu.VMEM((R, LANES), BF),
        pltpu.VMEM((R, LANES), BF),
        pltpu.VMEM((R, LANES), BF),
        pltpu.VMEM((16, D), F32),
        pltpu.VMEM((2, stages + 1, 8, D), F32),
        pltpu.VMEM((2, T // 2, D), F32),
        pltpu.VMEM((8, D, FC), BF),
        *[pltpu.VMEM((2 * nf + 2, n, FC), BF) for n in rows_at],
        *[pltpu.VMEM((3 * pairs, n, LANES), BF) for n in rows_at],
        dma((2 * nf + 2, stages)), dma((2 * nf + 2, stages)),
        dma((3 * pairs, stages)), dma((3 * pairs, stages)),
        dma((15,)), dma((15,)), dma((2, stages + 1)), dma((2, stages + 1)), dma((10 + 6 * pairs,)),
    ]
    n = D // dp
    struct = jax.ShapeDtypeStruct
    made = pl.pallas_call(
        functools.partial(kernel, dp),
        out_shape=(
            struct((T, D), BF), struct((T, D), F32), struct((n, F), F32), struct((n, F), F32),
            struct((n, E), F32), struct((3, n, E), F32), struct((16, D), F32),
        ),
        in_specs=[hbm] * 6 + [smem] + [vmem] * 9,
        out_specs=(hbm, hbm, vmem, vmem, vmem, vmem, vmem),
        scratch_shapes=scratch,
        compiler_params=pltpu.CompilerParams(
            collective_id=0, has_side_effects=True, vmem_limit_bytes=63 << 20
        ),
        name="block",
    )(
        tokens, cotangent, proj_weight, out_weight, up_weight, down_weight, episode_lengths,
        row(attn_gain), row(attn_shift), proj_bias, row(out_bias), row(mlp_gain), row(mlp_shift),
        row(up_bias), row(down_bias), jnp.asarray(rope_tables()),
    )
    vectors = [struct((1, D), F32)] * 6 + [struct((3, D), F32), struct((4, D), F32)]
    mixed, grad_tokens, down, up, out, proj, gain1, shift1, obias, gain2, shift2, dbias, pbias, ubias = pl.pallas_call(
        hand_over,
        out_shape=tuple(struct(v.shape, v.dtype) for v in made[:6]) + tuple(vectors),
        in_specs=[hbm] * 6 + [vmem],
        out_specs=(hbm,) * 6 + (vmem,) * 8,
        scratch_shapes=[*(pltpu.VMEM(v.shape, v.dtype) for v in made[:6]), dma((6,)), dma((6,))],
        name="outputs",
    )(*made)
    return (
        mixed, grad_tokens, gain1[0], shift1[0], proj, pbias, out.T, obias[0], gain2[0], shift2[0],
        up, ubias.reshape(-1), down.T, dbias[0],
    )


def solution(mesh):
    rows = P(("dp", "tensor"), None)
    return jax.shard_map(
        on_device,
        mesh=mesh,
        in_specs=(
            rows, P("dp", None), P(), P(), P(None, None, "tensor"), P(None, "tensor"), P("tensor", None), P(),
            P(), P(), P(None, "tensor"), P("tensor"), P("tensor", None), P(), rows,
        ),
        out_specs=(
            rows, rows, P(), P(), P(None, "dp", "tensor"), P(), P("tensor", "dp"), P(), P(), P(),
            P("dp", "tensor"), P(), P("tensor", "dp"), P(),
        ),
        check_vma=False,
    )
```

time: 235 us -> 177 us (0.75)
  Pallas kernels: 221 us -> 174 us
  local copies, waits for them, and re-layouts: 12.2 us -> 1.32 us
    pallas_call x1 -> x2, Pallas kernels: 221 us -> 174 us  [the longest x1 169 us: on_device(): pl.pallas_call(functools.partial(kernel, dp), out_shape=(struct((T, D), B...]
    transpose x2 -> x0, local copies, waits for them, and re-layouts: 4.2 us -> none  [the longest x1 2.41 us: on_device(): down = shard[:, :F].T]
    unnamed x9 -> x1, local copies, waits for them, and re-layouts: 4.96 us -> 1.32 us
    slice x2 -> x0, local copies, waits for them, and re-layouts: 3.02 us -> none  [the longest x1 1.56 us: on_device(): small[12]]
where the time goes in v2:
time: 177 us; the launch traced here: 176 us
  Pallas kernels  174 us (98%)
    pallas_call x1, Pallas kernels, on_device(): pl.pallas_call(functools.partial(kernel, dp), out_shape=(struct((T, D), B...  169 us
    pallas_call x1, Pallas kernels, on_device(): pl.pallas_call(hand_over, out_shape=tuple((struct(v.shape, v.dtype) for v...  5.33 us

profile of v2, /device:TPU:0, one launch (start us, length us, event | category | flops | bytes accessed | tf_op | source)
XLA Modules:
  0.0 176.3 jit_solution(14807698885177225449)
XLA Ops:
  0.7 169.0 %block.1 = (bf16[512,1024]{1,0:T(8,128)(2,1)}, f32[512,1024]{1,0:T(8,128)}, f32[64,2048]{1,0:T(8,128)}, f32[64,2048]{1,0:T(8,128)}, f32[64,512]{1,0:T(8,128)}, /...) custom-call(bf16[512,1024]{1,0:T(8,128)(2,1)} %tok_h.1, bf16[512,1024]{1,0:T(8,128)(2,1)} %cot_h.1, bf16[3,1024,512]{2,1,0:T(8,128)(2,1)} %pw_h.1, ...), custom_call_target="tpu_custom_call" | custom-call | tf_op jit(solution)/shard_map/block/pallas_call | solution.py:870
  169.6 5.3 %outputs.1 = (bf16[512,1024]{1,0:T(8,128)(2,1)}, f32[512,1024]{1,0:T(8,128)}, f32[64,2048]{1,0:T(8,128)}, f32[64,2048]{1,0:T(8,128)}, f32[64,512]{1,0:T(8,128)},...) custom-call(bf16[512,1024]{1,0:T(8,128)(2,1)} %get-tuple-element.35., ...), custom_call_target="tpu_custom_call" | custom-call | tf_op jit(solution)/shard_map/outputs/pallas_call | solution.py:889
  175.0 1.3 copy.32

commit v3 on v2

--- a/solution.py
+++ b/solution.py
@@ -615,10 +615,10 @@
         def _(m):
             three = nn(T2[pl.ds(m * 512, 512)], GH[:, own_cols])
             for c in range(3):
-                put("P", (p, c), three[:, c * LANES : (c + 1) * LANES], m, P_KINDS[c], 0)
+                put("P", (p, c), three[:, c * LANES : (c + 1) * LANES], m, P_KINDS[c], p % 2)
 
         for c in range(3):
-            rs_start("P", (p, c), 0, order_of(P_KINDS[c], 0))
+            rs_start("P", (p, c), 0, order_of(P_KINDS[c], p % 2))
         totals = nn(ones8, GH[:, own_cols])[0:1]
         for c in range(3):
             at = pl.multiple_of(core * E + p * LANES, LANES)
@@ -699,26 +699,39 @@
         gtok_store(m).wait()
 
 
+def pieces_of(shapes):
+    parts = []
+    for k, shape in enumerate(shapes):
+        n = math.gcd(shape[0], 64)
+        parts += [(k, at, n) for at in range(0, shape[0], n)]
+    return parts
+
+
 def hand_over(*refs):
-    arrive = [pltpu.make_async_copy(refs[k], refs[-8 + k], refs[-2].at[k]) for k in range(6)]
-    leave = [pltpu.make_async_copy(refs[-8 + k], refs[7 + k], refs[-1].at[k]) for k in range(6)]
+    parts = pieces_of([ref.shape for ref in refs[:6]])
+    arrive, leave = [], []
+    for q, (k, at, n) in enumerate(parts):
+        rows = pl.ds(at, n)
+        arrive.append(pltpu.make_async_copy(refs[k].at[rows], refs[-8 + k].at[rows], refs[-2].at[q]))
+        leave.append(pltpu.make_async_copy(refs[-8 + k].at[rows], refs[7 + k].at[rows], refs[-1].at[q]))
     for c in arrive:
         c.start()
     small, vectors = refs[6], refs[13:21]
     for v, at in zip(vectors, (0, 1, 8, 9, 10, 15)):
         v[...] = small[at : at + 1]
     vectors[6][...] = small[2:5]
-    vectors[7][...] = small[11:15]
-    for k in range(6):
-        arrive[k].wait()
-        leave[k].start()
+    for k in range(4):
+        vectors[7][:, k * small.shape[1] : (k + 1) * small.shape[1]] = small[11 + k : 12 + k]
+    for before, after in zip(arrive, leave):
+        before.wait()
+        after.start()
     for c in leave:
         c.wait()
 
 
 M_KINDS = ("xyz", "yzx", "zxy", "yxz")
-O_KINDS = ("xzy", "zyx")
-P_KINDS = ("xyz", "yzx", "zxy")
+O_KINDS = ("xyz", "yzx")
+P_KINDS = ("xyz", "yxz", "zxy")
 
 
 def kind_of(fam, c):
@@ -726,7 +739,7 @@
         return M_KINDS[2 * (c[0] % 2) + c[1]], (c[0] // 2) % 2
     if fam == "O":
         return O_KINDS[c], 0
-    return P_KINDS[c[1]], 0
+    return P_KINDS[c[1]], c[0] % 2
 
 
 def make_plan(stages, nf, pairs):
@@ -805,8 +818,8 @@
     return plan
 
 
-WIRE = 8.0
-LATENCY = 6.0
+WIRE = 8.5
+LATENCY = 5.0
 SLACK = 0.0
 STEP = 0.3
 TIMES = dict(
@@ -885,13 +898,14 @@
         row(attn_gain), row(attn_shift), proj_bias, row(out_bias), row(mlp_gain), row(mlp_shift),
         row(up_bias), row(down_bias), jnp.asarray(rope_tables()),
     )
-    vectors = [struct((1, D), F32)] * 6 + [struct((3, D), F32), struct((4, D), F32)]
+    parts = len(pieces_of([v.shape for v in made[:6]]))
+    vectors = [struct((1, D), F32)] * 6 + [struct((3, D), F32), struct((1, 4 * D), F32)]
     mixed, grad_tokens, down, up, out, proj, gain1, shift1, obias, gain2, shift2, dbias, pbias, ubias = pl.pallas_call(
         hand_over,
         out_shape=tuple(struct(v.shape, v.dtype) for v in made[:6]) + tuple(vectors),
         in_specs=[hbm] * 6 + [vmem],
         out_specs=(hbm,) * 6 + (vmem,) * 8,
-        scratch_shapes=[*(pltpu.VMEM(v.shape, v.dtype) for v in made[:6]), dma((6,)), dma((6,))],
+        scratch_shapes=[*(pltpu.VMEM(v.shape, v.dtype) for v in made[:6]), dma((parts,)), dma((parts,))],
         name="outputs",
     )(*made)
     return (

time: 177 us -> 177 us (level)
  Pallas kernels: 174 us -> 176 us
where the time goes in v3:
time: 177 us
  Pallas kernels  176 us (99%)
    pallas_call x1, Pallas kernels, on_device(): pl.pallas_call(functools.partial(kernel, dp), out_shape=(struct((T, D), B...  170 us
    pallas_call x1, Pallas kernels, on_device(): pl.pallas_call(hand_over, out_shape=tuple((struct(v.shape, v.dtype) for v...  6.16 us

profile of v3, /device:TPU:0, one launch (start us, length us, event | category | flops | bytes accessed | tf_op | source)
XLA Modules:
  0.0 176.8 jit_solution(8183990135276075561)
XLA Ops:
  0.7 169.8 %block.1 = (bf16[512,1024]{1,0:T(8,128)(2,1)}, f32[512,1024]{1,0:T(8,128)}, f32[64,2048]{1,0:T(8,128)}, f32[64,2048]{1,0:T(8,128)}, f32[64,512]{1,0:T(8,128)}, /...) custom-call(bf16[512,1024]{1,0:T(8,128)(2,1)} %tok_h.1, bf16[512,1024]{1,0:T(8,128)(2,1)} %cot_h.1, bf16[3,1024,512]{2,1,0:T(8,128)(2,1)} %pw_h.1, ...), custom_call_target="tpu_custom_call" | custom-call | tf_op jit(solution)/shard_map/block/pallas_call | solution.py:883
  170.4 6.2 %outputs.1 = (bf16[512,1024]{1,0:T(8,128)(2,1)}, f32[512,1024]{1,0:T(8,128)}, f32[64,2048]{1,0:T(8,128)}, f32[64,2048]{1,0:T(8,128)}, f32[64,512]{1,0:T(8,128)},...) custom-call(bf16[512,1024]{1,0:T(8,128)(2,1)} %get-tuple-element.35., ...), custom_call_target="tpu_custom_call" | custom-call | tf_op jit(solution)/shard_map/outputs/pallas_call | solution.py:903
